TPU v7x, 256 devices: a whole 4x4x8 slice. The times are simulated.
256 devices in a mesh: band: 128 (over z, y, x), tp: 2 (over core).
Axes of the slice: x: 4, y: 4, z: 8, core: 2. Of those that a mesh axis runs over, the one named last changes fastest.
Arguments:
- grid_input: bfloat16 [131072, 474], P('band'), may hold values from -6 to 6
- mesh_latent: bfloat16 [40960, 512], P('band'), may hold values from -6 to 6
- edge_latent: bfloat16 [327680, 512], P('band'), may hold values from -6 to 6
- slot_grid_row: int32 [384, 1024], P('band'), may hold values from 0 to 1024, as said below
- slot_mesh_row: int32 [384, 1024], P('band'), may hold values from 0 to 320, as said below
- halo_send: int32 [16384, 16], P('band'), may hold values from 0 to 320, as said below
- edge_sender: int32 [327680], P('band'), may hold values from 0 to 2367, as said below
- edge_receiver: int32 [327680], P('band'), may hold values from 0 to 319
- embed_in: bfloat16 [474, 512], P(None, 'tp'), may hold values from -0.25 to 0.25
- embed_out: bfloat16 [512, 512], P('tp'), may hold values from -0.25 to 0.25
- encode_sender: bfloat16 [512, 512], P(None, 'tp'), may hold values from -0.25 to 0.25
- encode_receiver: bfloat16 [512, 512], P(None, 'tp'), may hold values from -0.25 to 0.25
- encode_out: bfloat16 [512, 512], P('tp'), may hold values from -0.25 to 0.25
- encode_node_in: bfloat16 [1024, 512], P(None, 'tp'), may hold values from -0.1875 to 0.1875
- encode_node_out: bfloat16 [512, 512], P('tp'), may hold values from -0.25 to 0.25
- layer_sender: bfloat16 [2, 512, 512], P(None, None, 'tp'), may hold values from -0.25 to 0.25
- layer_receiver: bfloat16 [2, 512, 512], P(None, None, 'tp'), may hold values from -0.25 to 0.25
- layer_edge: bfloat16 [2, 512, 512], P(None, None, 'tp'), may hold values from -0.25 to 0.25
- layer_message: bfloat16 [2, 512, 512], P(None, 'tp'), may hold values from -0.25 to 0.25
- layer_node_in: bfloat16 [2, 1024, 512], P(None, None, 'tp'), may hold values from -0.1875 to 0.1875
- layer_node_out: bfloat16 [2, 512, 512], P(None, 'tp'), may hold values from -0.25 to 0.25
Outputs:
- mesh_result: bfloat16 [40960, 512], P('band')
Inputs may be any that keep to these rules, and one draw needn't show every extreme that they name: `slot_grid_row`: 1024 marks an empty slot; live slots of a block come first; block 0 of the first band and block 2 of the last are empty; every other block holds 256 to 1024 live slots, and in every draw all three blocks sending to some partition are full. `slot_mesh_row`: 320 marks an empty slot, exactly where the matching sending slot is empty. `halo_send`: 320 marks an empty slot; live slots come first; a partition sends nothing to itself; in every draw some partition receives 16 live slots from every other. `edge_sender`: a value s at or over 320 names slot (s - 320) % 16 sent by partition (s - 320) // 16 to this one, always a live slot.
All inputs are finite; a program needn't handle non-finite values.
Results may differ from a plain program's by a relative error of at most 0.028.
Values may be sent and summed in bfloat16 or wider, within the bound.
No kernel may reach another device: no remote copies, remote signals or barrier semaphores. Data moves between devices by JAX's collectives and lax.ppermute only.
A program may use at most 64 MiB of HBM per device.

v0:
```python
import functools

import jax
import jax.numpy as jnp
from jax import lax
from jax.experimental import pallas as pl
from jax.experimental.pallas import tpu as pltpu
from jax.sharding import PartitionSpec as P

BF16 = jnp.bfloat16
F32 = jnp.float32


def matmul(left, right, left_dim=1, right_dim=0):
    dims = (((left_dim,), (right_dim,)), ((), ()))
    return lax.dot_general(left, right, dims, preferred_element_type=F32)


def silu(values):
    half = 0.5 * values
    return half + half * jnp.tanh(half)


def normalize(values, axis):
    centre = jnp.mean(values, axis=axis, keepdims=True)
    centered = values - centre
    variance = jnp.mean(centered * centered, axis=axis, keepdims=True)
    return centered * lax.rsqrt(variance + 1e-05)


def as_column(row):
    return jnp.transpose(jnp.broadcast_to(row, (128, row.shape[1])))


def pick_rows(column, count):
    n = column.shape[0]
    wide = jnp.concatenate([column] * pl.cdiv(count, 128), axis=1)[:, :count]
    lanes = lax.broadcasted_iota(jnp.int32, (n, count), 1)
    return jnp.where(wide == lanes, 1.0, 0.0).astype(BF16)


def pick_columns(row, count):
    n = row.shape[1]
    rows = lax.broadcasted_iota(jnp.int32, (count, n), 0)
    return jnp.where(row == rows, 1.0, 0.0).astype(BF16)


class Carry:
    def __init__(self, array, layer=None, used=False):
        self.array, self.layer, self.used, self.pieces = array, layer, used, 1
        self.shape = array.shape if layer is None else array.shape[1:]


class Layer:
    def __init__(self, array, layer):
        self.array, self.layer = array, layer


class Far:
    def __init__(self, array, layer=None, pieces=1):
        self.array, self.layer, self.pieces = array, layer, pieces
        self.shape = array.shape if layer is None else array.shape[1:]


class Incoming:
    def __init__(self, spec, ref, held, sems, first):
        self.source = ref if spec.layer is None else ref.at[spec.layer]
        self.held, self.sems, self.first = held, sems, first
        self.shape, self.pieces, self.rows = spec.shape, spec.pieces, spec.shape[0] // spec.pieces
        self.waiting = True
        for index in range(self.pieces):
            self.copy(index).start()

    def copy(self, index):
        rows = pl.ds(index * self.rows, self.rows)
        sem = self.sems.at[self.first + index]
        return pltpu.make_async_copy(self.source.at[rows], self.held.at[rows], sem)

    def piece(self, index):
        self.waiting = False
        self.copy(index).wait()
        return self.held[pl.ds(pl.multiple_of(index * self.rows, self.rows), self.rows), :]

    def wait(self):
        if self.waiting:
            self.waiting = False
            for index in range(self.pieces):
                self.copy(index).wait()

    def __getitem__(self, key):
        self.wait()
        return self.held[key]


class Outgoing:
    def __init__(self, ref, held, sems, first, pieces):
        self.ref, self.held, self.sems, self.first = ref, held, sems, first
        self.pieces, self.rows = pieces, ref.shape[0] // pieces

    def copy(self, index):
        rows = pl.ds(index * self.rows, self.rows)
        sem = self.sems.at[self.first + index]
        return pltpu.make_async_copy(self.held.at[rows], self.ref.at[rows], sem)

    def put(self, index, values):
        self.held[pl.ds(pl.multiple_of(index * self.rows, self.rows), self.rows), :] = values
        self.copy(index).start()

    def wait(self):
        for index in range(self.pieces):
            self.copy(index).wait()


def call(kernel, outs, *args, extra=()):
    scratch, semaphores = [], 0
    for arg in args:
        if isinstance(arg, Far):
            scratch.append(pltpu.VMEM(arg.shape, arg.array.dtype))
            semaphores += arg.pieces
    for shape, dtype, pieces in outs:
        if pieces:
            scratch.append(pltpu.VMEM(shape, dtype))
            semaphores += pieces
    carried = [arg for arg in args if isinstance(arg, Carry)]
    semaphores += len(carried)
    all_outs = list(outs) + [(arg.shape, arg.array.dtype, 0) for arg in carried]

    def body(*refs):
        inputs, refs = refs[: len(args)], refs[len(args) :]
        results, held = refs[: len(all_outs)], list(refs[len(all_outs) : -1])
        held, own = held[: len(held) - len(extra)], held[len(held) - len(extra) :]
        sems, first = refs[-1], 0
        copied = list(results[len(outs) :])
        taken, given, carries = [], [], []
        for arg, ref in zip(args, inputs):
            if isinstance(arg, Far):
                taken.append(Incoming(arg, ref, held.pop(0), sems, first))
                first += arg.pieces
            elif isinstance(arg, Carry):
                carries.append((arg, ref, copied.pop(0), first))
                if arg.used:
                    taken.append(Incoming(arg, ref, carries[-1][2], sems, first))
                first += 1
            else:
                taken.append(ref.at[arg.layer] if isinstance(arg, Layer) else ref)
        carries = [Incoming(*each[:3], sems, each[3]) for each in carries if not each[0].used]
        for (shape, dtype, pieces), ref in zip(outs, results):
            if pieces:
                ref = Outgoing(ref, held.pop(0), sems, first, pieces)
                first += pieces
            given.append(ref)
        kernel(*taken, *given, *own)
        for ref in taken + carries + given:
            if isinstance(ref, (Incoming, Outgoing)):
                ref.wait()

    def space(far):
        return pl.BlockSpec(memory_space=pltpu.HBM if far else pltpu.VMEM)

    def operand(arg):
        if isinstance(arg, (Far, Carry)):
            return pltpu.with_memory_space_constraint(arg.array, pltpu.HBM)
        return arg.array if isinstance(arg, Layer) else arg

    return pl.pallas_call(
        body,
        out_shape=[
            pltpu.HBM(shape, dtype) if pieces else jax.ShapeDtypeStruct(shape, dtype)
            for shape, dtype, pieces in all_outs
        ],
        in_specs=[space(isinstance(arg, (Far, Carry))) for arg in args],
        out_specs=[space(pieces > 0) for _, _, pieces in all_outs],
        scratch_shapes=scratch + list(extra) + [pltpu.SemaphoreType.DMA((max(semaphores, 1),))],
        compiler_params=pltpu.CompilerParams(vmem_limit_bytes=32 * 1024 * 1024),
    )(*[operand(arg) for arg in args])


def each_block(count, block, body, init=None, unroll=1):
    def step(index, carry):
        return body(pl.ds(pl.multiple_of(index * block, block), block), index, carry)

    return lax.fori_loop(0, count // block, step, init, unroll=unroll)


def embed_own_kernel(block, x, in_own, own_ref):
    weight = in_own[...]
    x.wait()

    def step(columns, index, carry):
        own_ref[:, columns] = silu(matmul(weight, x[:, columns], 0)).astype(BF16)

    each_block(x.shape[1], block, step)


def embed_kernel(block, x, own, in_other, out_own, out_other, sender_own, sender_other, slots, send_ref,
                 proj_ref):
    half = sender_own.shape[1]

    def embed(columns, index, carry):
        other = silu(matmul(in_other[...], x[:, columns], 0)).astype(BF16)
        total = matmul(out_own[...], own[:, columns], 0) + matmul(out_other[...], other, 0)
        latent = normalize(total, 0).astype(BF16)
        proj_ref[:half, columns] = matmul(sender_own[...], latent, 0).astype(BF16)
        proj_ref[half:, columns] = matmul(sender_other[...], latent, 0).astype(BF16)

    each_block(x.shape[1], block, embed, unroll=True)
    slots.wait()

    def gather(columns, index, carry):
        low = lax.axis_index("tp") == 0
        row = jnp.where(low, slots[2:3, columns], slots[0:1, columns])
        pick = pick_columns(row, proj_ref.shape[1])
        send_ref[:, columns] = matmul(proj_ref[...], pick).astype(BF16)

    each_block(send_ref.shape[1], block, gather, unroll=True)


def join(incoming, row, mesh_proj):
    pick = pick_columns(row, mesh_proj.shape[1])
    active = silu(incoming + matmul(mesh_proj, pick)).astype(BF16)
    return matmul(pick, jnp.transpose(active))


def prepare(latent, msg_own, msg_other, first_own, first_other, base_ref, fold_ref):
    width = latent.shape[1]
    firsts = (first_own, first_other)
    base_ref.put(0, jnp.concatenate([matmul(latent, each[:width, :]) for each in firsts], axis=1))
    fold = [
        jnp.concatenate([matmul(msg[...], each[width:, :]) for each in firsts], axis=1)
        for msg in (msg_own, msg_other)
    ]
    fold_ref.put(0, jnp.concatenate(fold, axis=0).astype(BF16))


def encode_mid_kernel(block, latent, receiver_own, receiver_other, grid_slots, mesh_slots, grid_proj,
                      msg_own, msg_other, first_own, first_other, proj_ref, sum_ref, base_ref,
                      fold_ref):
    nodes = latent[...]
    half = receiver_own.shape[1]
    proj_ref[:half, :] = matmul(receiver_own[...], nodes, 0, 1).astype(BF16)
    proj_ref[half:, :] = matmul(receiver_other[...], nodes, 0, 1).astype(BF16)
    low = lax.axis_index("tp") == 0
    middle = grid_slots.shape[1] // 2
    grid_row, mesh_row = [
        jnp.where(low, each[1:2, :middle], each[1:2, middle:]) for each in (grid_slots, mesh_slots)
    ]
    incoming = matmul(grid_proj[...], pick_columns(grid_row, grid_proj.shape[1]))
    sum_ref[...] = join(incoming, mesh_row, proj_ref[...])
    prepare(nodes, msg_own, msg_other, first_own, first_other, base_ref, fold_ref)


def encode_far_kernel(block, mesh_proj, partial, mesh_slots, arrived, sum_ref, total_ref):
    total_ref[...] = partial[...]
    mesh_slots.wait()

    def step(columns, index, carry):
        low = lax.axis_index("tp") == 0
        row = jnp.where(low, mesh_slots[0:1, columns], mesh_slots[2:3, columns])
        total_ref[...] += join(arrived[:, columns].astype(F32), row, mesh_proj[...])

    each_block(arrived.shape[1], block, step, unroll=True)
    sum_ref[...] = total_ref[...].astype(BF16)


def node_kernel(hidden_own, hidden_other, fold, base, second_own, second_other, latent, *refs):
    half = second_own.shape[0]
    own, other = hidden_own[...], hidden_other[...]
    if own.shape[1] > half:
        mine, theirs = own.astype(F32), other.astype(F32)
        own = (mine[:, :half] + theirs[:, half:]).astype(BF16)
        other = (mine[:, half:] + theirs[:, :half]).astype(BF16)
    pre_act = matmul(own, fold[:half, :]) + matmul(other, fold[half:, :])
    inner = silu(base[...] + pre_act).astype(BF16)
    total = matmul(inner[:, :half], second_own[...]) + matmul(inner[:, half:], second_other[...])
    new = (latent[...].astype(F32) + normalize(total, 1)).astype(BF16)
    if len(refs) == 1:
        refs[0][...] = new
        return
    sender_w, halo, new_ref, outgoing_ref = refs
    new_ref.put(0, new)
    local = matmul(new, sender_w[...]).astype(BF16)

    def step(columns, index, carry):
        pick = pick_rows(as_column(halo[:, columns]), local.shape[0])
        outgoing_ref.put(index, matmul(pick, local).astype(BF16))

    each_block(halo.shape[1], outgoing_ref.rows, step, unroll=True)


def edge_near_kernel(latent, sender_w, receiver_w, edge_w, edges, senders, receivers, msg_own,
                     msg_other, first_own, first_other, near_ref, base_ref, fold_ref):
    nodes = latent[...]
    count = nodes.shape[0]
    table = [matmul(each[...], nodes, 0, 1).astype(BF16) for each in (sender_w, receiver_w)]
    table = jnp.concatenate(table, axis=1)
    weight = edge_w[...]

    def step(columns, index, carry):
        pick = jnp.concatenate(
            [pick_columns(each[:, columns], count) for each in (senders, receivers)], axis=0
        )
        near = matmul(weight, edges.piece(index), 0, 1) + matmul(table, pick)
        near_ref.put(index, near.astype(BF16))

    each_block(edges.shape[0], edges.rows, step)
    prepare(nodes, msg_own, msg_other, first_own, first_other, base_ref, fold_ref)


def edge_far_kernel(count, arrived, near, senders, receivers, hidden_ref):
    far = arrived.shape[0]
    table = jnp.transpose(arrived[...])

    def step(columns, index, total):
        pre_act = matmul(table, pick_columns(senders[:, columns] - count, far))
        pre_act = near.piece(index).astype(F32) + pre_act
        pick = pick_columns(receivers[:, columns], count)
        return total + matmul(pick, jnp.transpose(silu(pre_act).astype(BF16)))

    total = each_block(senders.shape[1], near.shape[1], step, jnp.zeros(hidden_ref.shape, F32))
    hidden_ref[...] = total.astype(BF16)


def swap(values):
    return lax.ppermute(values, "tp", [(0, 1), (1, 0)])


def shards(
    grid_input,
    mesh_latent,
    edge_latent,
    slot_grid_row,
    slot_mesh_row,
    halo_send,
    edge_sender,
    edge_receiver,
    embed_in,
    embed_out,
    encode_sender,
    encode_receiver,
    encode_out,
    encode_node_in,
    encode_node_out,
    layer_sender,
    layer_receiver,
    layer_edge,
    layer_message,
    layer_node_in,
    layer_node_out,
):
    nodes, width = mesh_latent.shape
    grid_rows = grid_input.shape[0]
    slot_count = slot_grid_row.shape[1]
    half = encode_sender.shape[1]
    bands, halo_slots = halo_send.shape
    layers = layer_sender.shape[0]
    pieces = 5
    block = 512
    edge_rows = edge_latent.shape[0] // pieces

    own, x, out_own, sender_own = call(
        functools.partial(embed_own_kernel, block), [((half, grid_rows), BF16, 0)], Carry(grid_input.T, None, True),
        Far(embed_in), Carry(embed_out), Carry(encode_sender),
    )
    outgoing, grid_proj = call(
        functools.partial(embed_kernel, block),
        [((width, slot_count), BF16, 0), ((width, grid_rows), BF16, 0)], x, own, swap(embed_in),
        out_own, swap(embed_out), sender_own, swap(encode_sender), Far(slot_grid_row),
    )
    pairs = [(2 * i, 2 * i + 2) for i in range(bands - 1)]
    pairs += [(2 * i + 3, 2 * i + 1) for i in range(bands - 1)]
    arrived = lax.ppermute(outgoing, ("band", "tp"), pairs)

    owned = (encode_receiver, encode_out, encode_node_in, encode_node_out, layer_message,
             layer_node_in, layer_node_out)
    owned, grid_proj = lax.optimization_barrier((owned, grid_proj))
    receiver, encode_message, encode_first, encode_second, message, first, second = [
        (each, swap(each)) for each in owned
    ]

    def prepare_weights(message, first, layer):
        return [Far(each, layer) for pair in (message, first) for each in pair]

    prepared = [((nodes, width), F32, 1), ((width, width), BF16, 1)]
    mesh_proj, partial, base, fold = call(
        functools.partial(encode_mid_kernel, block),
        [((width, nodes), BF16, 0), ((nodes, width), F32, 0)] + prepared,
        Far(mesh_latent), Far(receiver[0]), Far(receiver[1]), Far(slot_grid_row),
        Far(slot_mesh_row), grid_proj, *prepare_weights(encode_message, encode_first, None),
    )
    hidden, *update, sender_w = call(
        functools.partial(encode_far_kernel, block), [((nodes, width), BF16, 0)], mesh_proj,
        partial, Far(slot_mesh_row), arrived, Carry(fold), Carry(base), Carry(encode_second[0]),
        Carry(encode_second[1]), Carry(mesh_latent), Carry(layer_sender, 0),
        extra=[pltpu.VMEM((nodes, width), F32)],
    )

    halo_row = halo_send.reshape(1, -1)
    sender_row = edge_sender.reshape(1, -1)
    receiver_row = edge_receiver.reshape(1, -1)
    node_out = [((nodes, width), BF16, 1), ((bands * halo_slots, half), BF16, 4)]

    for layer in range(layers):
        latent, outgoing = call(
            node_kernel, node_out, hidden, swap(hidden), *update, sender_w, halo_row
        )
        arrived = lax.all_to_all(
            outgoing.reshape(bands, halo_slots, half), "band", split_axis=0, concat_axis=0, tiled=True
        ).reshape(bands * halo_slots, half)
        near, base, fold = call(
            edge_near_kernel, [((pieces * half, edge_rows), BF16, pieces)] + prepared, Far(latent),
            Far(layer_sender, layer), Far(layer_receiver, layer), Far(layer_edge, layer),
            Far(edge_latent, None, pieces), sender_row, receiver_row,
            *prepare_weights(message, first, layer),
        )
        (hidden,) = call(
            functools.partial(edge_far_kernel, nodes), [((nodes, half), BF16, 0)], arrived,
            Far(near, None, pieces), sender_row, receiver_row,
        )
        update = [fold, base, Layer(second[0], layer), Layer(second[1], layer), latent]
        if layer + 1 < layers:
            sender_w = Layer(layer_sender, layer + 1)
    (latent,) = call(node_kernel, [((nodes, width), BF16, 0)], hidden, swap(hidden), *update)
    return latent


def solution(mesh):
    return jax.shard_map(
        shards,
        mesh=mesh,
        in_specs=(
            P("band", None),
            P("band", None),
            P("band", None),
            P("band", None),
            P("band", None),
            P("band", None),
            P("band"),
            P("band"),
            P(None, "tp"),
            P("tp", None),
            P(None, "tp"),
            P(None, "tp"),
            P("tp", None),
            P(None, "tp"),
            P("tp", None),
            P(None, None, "tp"),
            P(None, None, "tp"),
            P(None, None, "tp"),
            P(None, "tp", None),
            P(None, None, "tp"),
            P(None, "tp", None),
        ),
        out_specs=P("band", None),
        check_vma=False,
    )
```

profile of v0, /device:TPU:1, one launch (start us, length us, event | category | flops | bytes accessed | tf_op | source)
XLA Modules:
  0.0 139.1 jit_solution(12361610875192705419)
XLA Ops:
  0.0 3.2 %collective-permute-start.1 = (bf16[256,512]{1,0:T(8,128)(2,1)}, bf16[256,512]{1,0:T(8,128)(2,1)S(1)}, u32[]{:S(2)}, u32[]{:S(2)}) collective-permute-start(bf16[256,512]{1,0:T(8,128)(2,1)} %refs_2_.4), channel_id=1, source_target_pairs={{0,1},{1,0},{2,3},{3,2},{4,5},{5,4},{6,7},{7,6},{8,9},{9,8},{10,11... | collective-permute-start | bytes 786440 | tf_op jit(solution)/shard_map/ppermute | solution.py:324
  3.2 0.0 collective-permute-start.2
  3.2 0.5 collective-permute-start
  3.8 2.1 %shard_map.199 = (bf16[256,1024]{1,0:T(8,128)(2,1)S(1)}, bf16[474,1024]{1,0:T(8,128)(2,1)S(1)}, bf16[256,512]{1,0:T(8,128)(2,1)S(1)}, bf16[512,256]{1,0:T(8,128)(2,1)S(1)}) custom-call(bf16[474,1024]{1,0:T(8,128)(2,1)} %bitcast.9, bf16[474,256]{1,0:T(8,128)(2,1)} %refs_1_.3, bf16[256,512]{1,0:T(8,128)(2,1)} %refs_2_.4, bf16[512,256]{1,0:T(8,128)(2,1)} %refs_3_.4), custom_call_target="tpu_custom_call" | custom-call | tf_op jit(solution)/shard_map/pallas_call | solution.py:165
  5.8 0.0 collective-permute-done.refs_2_
  5.8 0.0 collective-permute-done.1.refs_4_
  5.8 0.0 collective-permute-done.2.refs_6_
  5.8 0.0 copy-start.11
  5.9 0.0 copy-start.15
  5.9 0.0 copy-start.16
  5.9 0.0 copy-start.13
  5.9 3.9 %shard_map.200 = (bf16[512,1024]{1,0:T(8,128)(2,1)S(1)}, bf16[512,1024]{1,0:T(8,128)(2,1)S(1)}) custom-call(bf16[474,1024]{1,0:T(8,128)(2,1)S(1)} %get-tuple-element.40.refs_0_, bf16[256,1024]{1,0:T(8,128)(2,1)S(1)} %get-tuple-element.41.refs_1_, bf16[474,256]{1,0:T(8,128)(2,1)S(1)} %collective-permute-done.refs_2_, ...), custom_call_target="tpu_custom_call" | custom-call | tf_op jit(solution)/shard_map/pallas_call | solution.py:165
  9.8 1.3 collective-permute-start.6
  11.1 0.5 collective-permute-start.5
  11.6 0.1 collective-permute-start.3
  11.7 0.4 collective-permute-start.4
  12.2 0.1 collective-permute-start.7
  12.3 1.3 collective-permute-done.3.refs_2_
  13.6 0.4 collective-permute-done.4.refs_7_
  13.9 0.0 collective-permute-done.5.refs_9_
  13.9 0.3 copy-done.17
  14.3 0.4 copy-done.18
  14.6 0.8 copy-done.12
  15.4 5.3 %shard_map.201 = (bf16[512,320]{1,0:T(8,128)(2,1)S(1)}, f32[320,512]{1,0:T(8,128)S(1)}, f32[320,512]{1,0:T(8,128)}, bf16[512,512]{1,0:T(8,128)(2,1)}) custom-call(bf16[320,512]{1,0:T(8,128)(2,1)} %refs_8_.2, bf16[512,256]{1,0:T(8,128)(2,1)} %refs_1_.4, bf16[512,256]{1,0:T(8,128)(2,1)} %copy-done.17, s32[3,1024]{1,0:T(4,128)} %refs_3_.5, s32[3,1024]{1,0:T(4,128)} %refs_2_.5, ...), custom_call_target="tpu_custom_call" | custom-call | tf_op jit(solution)/shard_map/pallas_call | solution.py:165
  20.7 0.0 collective-permute-done.7.refs_7_
  20.7 0.0 copy-start.14
  20.7 4.6 %collective-permute-done.6.refs_3_ = bf16[512,1024]{1,0:T(8,128)(2,1)S(1)} collective-permute-done((bf16[512,1024]{1,0:T(8,128)(2,1)S(1)}, bf16[512,1024]{1,0:T(8,128)(2,1)S(1)}, u32[]{:S(2)}, u32[]{:S(2)}) %collective-permute-start.6) | collective-permute-done | bytes 1048608 | tf_op jit(solution)/shard_map/ppermute | solution.py:371
  25.4 2.3 %shard_map.202 = (bf16[320,512]{1,0:T(8,128)(2,1)S(1)}, bf16[512,512]{1,0:T(8,128)(2,1)S(1)}, f32[320,512]{1,0:T(8,128)S(1)}, bf16[256,512]{1,0:T(8,128)(2,1)S(1...) custom-call(bf16[512,320]{1,0:T(8,128)(2,1)S(1)} %get-tuple-element.49.refs_0_, ...), custom_call_target="tpu_custom_call" | custom-call | tf_op jit(solution)/shard_map/pallas_call | solution.py:165
  27.7 0.3 collective-permute-start.8
  28.0 0.1 copy.23
  28.1 0.1 reshape.21.refs_8_
  28.2 1.4 %collective-permute-done.8.refs_1_ = bf16[320,512]{1,0:T(8,128)(2,1)S(1)} collective-permute-done((bf16[320,512]{1,0:T(8,128)(2,1)S(1)}, bf16[320,512]{1,0:T(8,128)(2,1)S(1)}, u32[]{:S(2)}, u32[]{:S(2)}) %collective-permute-start.8) | collective-permute-done | bytes 327712 | tf_op jit(solution)/shard_map/ppermute | solution.py:324
  29.6 2.7 %shard_map.203 = (bf16[320,512]{1,0:T(8,128)(2,1)}, bf16[2048,256]{1,0:T(8,128)(2,1)}) custom-call(bf16[320,512]{1,0:T(8,128)(2,1)S(1)} %get-tuple-element.55.refs_0_, bf16[320,512]{1,0:T(8,128)(2,1)S(1)} %collective-permute-done.8.refs_1_, bf16[512,512]{1,0:T(8,128)(2,1)S(1)} %get-tuple-element.56.refs_2_, f32[320,512]{1,0:T(8,128)S(1)} %get-tuple-element.57.refs_3_, ...), custom_call_target="tpu_custom_call" | custom-call | tf_op jit(solution)/shard_map/pallas_call | solution.py:165
  32.2 0.0 copy-start.9
  32.3 0.0 copy-start.1
  32.3 0.0 copy-start.19
  32.3 0.0 copy-start.20
  32.3 17.7 %all-to-all-start = ((bf16[128,16,256]{2,1,0:T(8,128)(2,1)}), bf16[128,16,256]{2,1,0:T(8,128)(2,1)S(1)}, u32[]{:S(2)}, u32[]{:S(2)}) async-start(bf16[128,16,256]{2,1,0:T(8,128)(2,1)} %bitcast.7), calls=%async_computation | async-start | bytes 2097152 | tf_op jit(solution)/shard_map/all_to_all | solution.py:406
  50.0 0.5 collective-permute-start.10
  50.5 0.1 collective-permute-start.9
  50.6 0.4 collective-permute-start.12
  51.0 0.0 copy-done.20
  51.1 2.5 %collective-permute-done.9.refs_8_ = bf16[2,256,512]{2,1,0:T(8,128)(2,1)S(1)} collective-permute-done((bf16[2,256,512]{2,1,0:T(8,128)(2,1)S(1)}, bf16[2,256,512]{2,1,0:T(8,128)(2,1)S(1)}, u32[]{:S(2)}, u32[]{:S(2)}) %collective-permute-start.9) | collective-permute-done | bytes 524320 | tf_op jit(solution)/shard_map/ppermute | solution.py:324
  53.5 0.0 collective-permute-done.10.refs_10_
  53.5 0.8 copy-done.10
  54.3 0.4 copy-done.8
  54.7 7.5 %shard_map.204 = (bf16[1280,512]{1,0:T(8,128)(2,1)}, f32[320,512]{1,0:T(8,128)}, bf16[512,512]{1,0:T(8,128)(2,1)}) custom-call(bf16[320,512]{1,0:T(8,128)(2,1)} %get-tuple-element.63.refs_0_.refs_6_, bf16[2,512,256]{2,1,0:T(8,128)(2,1)} %refs_1_.6, bf16[2,512,256]{2,1,0:T(8,128)(2,1)} %refs_2_.7, bf16[2,512,256]{2,1,0:T(8,128)(2,1)} %refs_3_.7, ...), custom_call_target="tpu_custom_call" | custom-call | tf_op jit(solution)/shard_map/pallas_call | solution.py:165
  62.2 0.0 copy-start
  62.2 0.0 copy-start.3
  62.3 17.2 %all-to-all-done = bf16[128,16,256]{2,1,0:T(8,128)(2,1)S(1)} async-done(((bf16[128,16,256]{2,1,0:T(8,128)(2,1)}), bf16[128,16,256]{2,1,0:T(8,128)(2,1)S(1)}, u32[]{:S(2)}, u32[]{:S(2)}) %all-to-all-start) | async-done | bytes 1048608 | tf_op jit(solution)/shard_map/all_to_all | solution.py:406
  79.5 5.9 %shard_map.205.refs_0_ = bf16[320,256]{1,0:T(8,128)(2,1)S(1)} custom-call(bf16[2048,256]{1,0:T(8,128)(2,1)S(1)} %bitcast.5, bf16[1280,512]{1,0:T(8,128)(2,1)} %get-tuple-element.66.refs_1_, s32[1,2560]{1,0:T(1,128)S(1)} %reshape.24.refs_5_.refs_2_, s32[1,2560]{1,0:T(1,128)S(1)} %reshape.25.refs_6_.refs_3_), custom_call_target="tpu_custom_call" | custom-call | tf_op jit(solution)/shard_map/pallas_call | solution.py:165
  85.3 2.9 %collective-permute-start.11 = (bf16[320,256]{1,0:T(8,128)(2,1)S(1)}, bf16[320,256]{1,0:T(8,128)(2,1)S(1)}, u32[]{:S(2)}, u32[]{:S(2)}) collective-permute-start(bf16[320,256]{1,0:T(8,128)(2,1)S(1)} %shard_map.205.refs_0_), channel_id=1, source_target_pairs={{0,1},{1,0},{2,3},{3,2},{4,5},{5,4},{6,7},{7,6},{8,9},{9,8},{10,11... | collective-permute-start | bytes 491528 | tf_op jit(solution)/shard_map/ppermute | solution.py:324
  88.2 0.0 collective-permute-done.12.refs_5_
  88.2 1.0 collective-permute-done.11.refs_1_
  89.2 0.0 copy-done
  89.3 2.6 %shard_map.206 = (bf16[320,512]{1,0:T(8,128)(2,1)}, bf16[2048,256]{1,0:T(8,128)(2,1)}) custom-call(bf16[320,256]{1,0:T(8,128)(2,1)S(1)} %shard_map.205.refs_0_, bf16[320,256]{1,0:T(8,128)(2,1)S(1)} %collective-permute-done.11.refs_1_, bf16[512,512]{1,0:T(8,128)(2,1)S(1)} %copy-done.7, f32[320,512]{1,0:T(8,128)S(1)} %copy-done.4, ...), custom_call_target="tpu_custom_call" | custom-call | tf_op jit(solution)/shard_map/pallas_call | solution.py:165
  91.9 6.4 %all-to-all-start.1 = ((bf16[128,16,256]{2,1,0:T(8,128)(2,1)}), bf16[128,16,256]{2,1,0:T(8,128)(2,1)S(1)}, u32[]{:S(2)}, u32[]{:S(2)}) async-start(bf16[128,16,256]{2,1,0:T(8,128)(2,1)} %bitcast.8), calls=%async_computation.1 | async-start | bytes 2097152 | tf_op jit(solution)/shard_map/all_to_all | solution.py:406
  98.3 7.5 %shard_map.207 = (bf16[1280,512]{1,0:T(8,128)(2,1)}, f32[320,512]{1,0:T(8,128)}, bf16[512,512]{1,0:T(8,128)(2,1)}) custom-call(bf16[320,512]{1,0:T(8,128)(2,1)} %get-tuple-element.71.refs_0_.refs_6_, bf16[2,512,256]{2,1,0:T(8,128)(2,1)} %refs_1_.6, bf16[2,512,256]{2,1,0:T(8,128)(2,1)} %refs_2_.7, bf16[2,512,256]{2,1,0:T(8,128)(2,1)} %refs_3_.7, ...), custom_call_target="tpu_custom_call" | custom-call | tf_op jit(solution)/shard_map/pallas_call | solution.py:165
  105.9 0.0 copy-start.2
  105.9 21.8 %all-to-all-done.1 = bf16[128,16,256]{2,1,0:T(8,128)(2,1)S(1)} async-done(((bf16[128,16,256]{2,1,0:T(8,128)(2,1)}), bf16[128,16,256]{2,1,0:T(8,128)(2,1)S(1)}, u32[]{:S(2)}, u32[]{:S(2)}) %all-to-all-start.1) | async-done | bytes 1048608 | tf_op jit(solution)/shard_map/all_to_all | solution.py:406
  127.7 5.9 %shard_map.208.refs_0_ = bf16[320,256]{1,0:T(8,128)(2,1)S(1)} custom-call(bf16[2048,256]{1,0:T(8,128)(2,1)S(1)} %bitcast.6, bf16[1280,512]{1,0:T(8,128)(2,1)} %get-tuple-element.72.refs_1_, s32[1,2560]{1,0:T(1,128)S(1)} %reshape.24.refs_5_.refs_2_, s32[1,2560]{1,0:T(1,128)S(1)} %reshape.25.refs_6_.refs_3_), custom_call_target="tpu_custom_call" | custom-call | tf_op jit(solution)/shard_map/pallas_call | solution.py:165
  133.6 2.8 %collective-permute-start.13 = (bf16[320,256]{1,0:T(8,128)(2,1)S(1)}, bf16[320,256]{1,0:T(8,128)(2,1)S(1)}, u32[]{:S(2)}, u32[]{:S(2)}) collective-permute-start(bf16[320,256]{1,0:T(8,128)(2,1)S(1)} %shard_map.208.refs_0_), channel_id=1, source_target_pairs={{0,1},{1,0},{2,3},{3,2},{4,5},{5,4},{6,7},{7,6},{8,9},{9,8},{10,11... | collective-permute-start | bytes 491528 | tf_op jit(solution)/shard_map/ppermute | solution.py:324
  136.3 1.0 collective-permute-done.13.refs_1_
  137.3 1.5 %shard_map.209 = bf16[320,512]{1,0:T(8,128)(2,1)} custom-call(bf16[320,256]{1,0:T(8,128)(2,1)S(1)} %shard_map.208.refs_0_, bf16[320,256]{1,0:T(8,128)(2,1)S(1)} %collective-permute-done.13.refs_1_, bf16[512,512]{1,0:T(8,128)(2,1)S(1)} %copy-done.6, f32[320,512]{1,0:T(8,128)S(1)} %copy-done.5, bf16[2,256,512]{2,1,0:T(8,128)(2,1)S(1)} %copy-done.1, ...), custom_call_target="tpu_custom_call" | custom-call | tf_op jit(solution)/shard_map/pallas_call | solution.py:165
  (27 shorter events, 0.1 us)
Async XLA Ops:
  0.0 5.8 %collective-permute-start.1 = (bf16[256,512]{1,0:T(8,128)(2,1)}, bf16[256,512]{1,0:T(8,128)(2,1)S(1)}, u32[]{:S(2)}, u32[]{:S(2)}) collective-permute-start(bf16[256,512]{1,0:T(8,128)(2,1)} %refs_2_.4), channel_id=1, source_target_pairs={{0,1},{1,0},{2,3},{3,2},{4,5},{5,4},{6,7},{7,6},{8,9},{9,8},{10,11... | collective-permute-start | bytes 786440 | tf_op jit(solution)/shard_map/ppermute | solution.py:324
  3.2 2.6 %collective-permute-start.2 = (bf16[512,256]{1,0:T(8,128)(2,1)}, bf16[512,256]{1,0:T(8,128)(2,1)S(1)}, u32[]{:S(2)}, u32[]{:S(2)}) collective-permute-start(bf16[512,256]{1,0:T(8,128)(2,1)} %refs_3_.4), channel_id=1, source_target_pairs={{0,1},{1,0},{2,3},{3,2},{4,5},{5,4},{6,7},{7,6},{8,9},{9,8},{10,11... | collective-permute-start | bytes 786440 | tf_op jit(solution)/shard_map/ppermute | solution.py:324
  3.2 2.6 %collective-permute-start = (bf16[474,256]{1,0:T(8,128)(2,1)}, bf16[474,256]{1,0:T(8,128)(2,1)S(1)}, u32[]{:S(2)}, u32[]{:S(2)}) collective-permute-start(bf16[474,256]{1,0:T(8,128)(2,1)} %refs_1_.3), channel_id=1, source_target_pairs={{0,1},{1,0},{2,3},{3,2},{4,5},{5,4},{6,7},{7,6},{8,9},{9,8},{10,11... | collective-permute-start | bytes 728072 | tf_op jit(solution)/shard_map/ppermute | solution.py:324
  5.8 5.3 %copy-start.11 = (bf16[1024,256]{1,0:T(8,128)(2,1)S(1)}, bf16[1024,256]{1,0:T(8,128)(2,1)}, u32[]{:S(2)}) copy-start(bf16[1024,256]{1,0:T(8,128)(2,1)} %refs_8_.1) | copy-start | bytes 1572868
  5.9 5.8 %copy-start.15 = (bf16[512,256]{1,0:T(8,128)(2,1)S(1)}, bf16[512,256]{1,0:T(8,128)(2,1)}, u32[]{:S(2)}) copy-start(bf16[512,256]{1,0:T(8,128)(2,1)} %refs_1_.4) | copy-start | bytes 786436
  5.9 5.9 %copy-start.16 = (bf16[256,512]{1,0:T(8,128)(2,1)S(1)}, bf16[256,512]{1,0:T(8,128)(2,1)}, u32[]{:S(2)}) copy-start(bf16[256,512]{1,0:T(8,128)(2,1)} %refs_6_) | copy-start | bytes 786436
  5.9 6.3 %copy-start.13 = (bf16[256,512]{1,0:T(8,128)(2,1)S(1)}, bf16[256,512]{1,0:T(8,128)(2,1)}, u32[]{:S(2)}) copy-start(bf16[256,512]{1,0:T(8,128)(2,1)} %refs_6_.1) | copy-start | bytes 786436
  9.8 15.5 %collective-permute-start.6 = (bf16[512,1024]{1,0:T(8,128)(2,1)S(1)}, bf16[512,1024]{1,0:T(8,128)(2,1)S(1)}, u32[]{:S(2)}, u32[]{:S(2)}) collective-permute-start(bf16[512,1024]{1,0:T(8,128)(2,1)S(1)} %get-tuple-element.51), channel_id=1, source_target_pairs={{0,2},{2,4},{4,6},{6,8},{8,10},{10,12},{12,14},{14,16},{16,18},{18... | collective-permute-start | bytes 3145736 | tf_op jit(solution)/shard_map/ppermute | solution.py:371
  11.1 2.8 %collective-permute-start.5 = (bf16[1024,256]{1,0:T(8,128)(2,1)S(1)}, bf16[1024,256]{1,0:T(8,128)(2,1)S(1)}, u32[]{:S(2)}, u32[]{:S(2)}) collective-permute-start(bf16[1024,256]{1,0:T(8,128)(2,1)S(1)} %copy-done.11), channel_id=1, source_target_pairs={{0,1},{1,0},{2,3},{3,2},{4,5},{5,4},{6,7},{7,6},{8,9},{9,8},{10,11... | collective-permute-start | bytes 1572872 | tf_op jit(solution)/shard_map/ppermute | solution.py:324
  11.6 1.9 %collective-permute-start.3 = (bf16[512,256]{1,0:T(8,128)(2,1)S(1)}, bf16[512,256]{1,0:T(8,128)(2,1)S(1)}, u32[]{:S(2)}, u32[]{:S(2)}) collective-permute-start(bf16[512,256]{1,0:T(8,128)(2,1)S(1)} %copy-done.15), channel_id=1, source_target_pairs={{0,1},{1,0},{2,3},{3,2},{4,5},{5,4},{6,7},{7,6},{8,9},{9,8},{10,11... | collective-permute-start | bytes 786440 | tf_op jit(solution)/shard_map/ppermute | solution.py:324
  11.7 2.2 %collective-permute-start.4 = (bf16[256,512]{1,0:T(8,128)(2,1)S(1)}, bf16[256,512]{1,0:T(8,128)(2,1)S(1)}, u32[]{:S(2)}, u32[]{:S(2)}) collective-permute-start(bf16[256,512]{1,0:T(8,128)(2,1)S(1)} %copy-done.16), channel_id=1, source_target_pairs={{0,1},{1,0},{2,3},{3,2},{4,5},{5,4},{6,7},{7,6},{8,9},{9,8},{10,11... | collective-permute-start | bytes 786440 | tf_op jit(solution)/shard_map/ppermute | solution.py:324
  12.2 8.6 %collective-permute-start.7 = (bf16[256,512]{1,0:T(8,128)(2,1)S(1)}, bf16[256,512]{1,0:T(8,128)(2,1)S(1)}, u32[]{:S(2)}, u32[]{:S(2)}) collective-permute-start(bf16[256,512]{1,0:T(8,128)(2,1)S(1)} %copy-done.13), channel_id=1, source_target_pairs={{0,1},{1,0},{2,3},{3,2},{4,5},{5,4},{6,7},{7,6},{8,9},{9,8},{10,11... | collective-permute-start | bytes 786440 | tf_op jit(solution)/shard_map/ppermute | solution.py:324
  13.5 0.7 copy-start.17
  13.9 0.7 copy-start.18
  14.6 0.8 copy-start.12
  20.7 4.6 %copy-start.14 = (bf16[256,512]{1,0:T(8,128)(2,1)}, bf16[256,512]{1,0:T(8,128)(2,1)S(1)}, u32[]{:S(2)}) copy-start(bf16[256,512]{1,0:T(8,128)(2,1)S(1)} %collective-permute-done.7.refs_7_) | copy-start | bytes 786436
  25.4 2.6 %copy-start.21 = (s32[128,16]{0,1:T(8,128)S(1)}, s32[128,16]{0,1:T(8,128)}, u32[]{:S(2)}) copy-start(s32[128,16]{0,1:T(8,128)} %param.26) | copy-start | bytes 24580
  27.7 1.9 %collective-permute-start.8 = (bf16[320,512]{1,0:T(8,128)(2,1)S(1)}, bf16[320,512]{1,0:T(8,128)(2,1)S(1)}, u32[]{:S(2)}, u32[]{:S(2)}) collective-permute-start(bf16[320,512]{1,0:T(8,128)(2,1)S(1)} %get-tuple-element.55.refs_0_), channel_id=1, source_target_pairs={{0,1},{1,0},{2,3},{3,2},{4,5},{5,4},{6,7},{7,6},{8,9},{9,8},{10,11... | collective-permute-start | bytes 983048 | tf_op jit(solution)/shard_map/ppermute | solution.py:324
  32.2 18.3 %copy-start.9 = (bf16[2,256,512]{2,1,0:T(8,128)(2,1)S(1)}, bf16[2,256,512]{2,1,0:T(8,128)(2,1)}, u32[]{:S(2)}) copy-start(bf16[2,256,512]{2,1,0:T(8,128)(2,1)} %refs_7_.5) | copy-start | bytes 1572868
  32.3 18.4 %copy-start.1 = (bf16[2,256,512]{2,1,0:T(8,128)(2,1)S(1)}, bf16[2,256,512]{2,1,0:T(8,128)(2,1)}, u32[]{:S(2)}) copy-start(bf16[2,256,512]{2,1,0:T(8,128)(2,1)} %refs_4_.7) | copy-start | bytes 1572868
  32.3 18.7 %copy-start.19 = (s32[2560]{0:T(1024)S(1)}, s32[2560]{0:T(1024)}, u32[]{:S(2)}) copy-start(s32[2560]{0:T(1024)} %param.27) | copy-start | bytes 30724
  32.3 18.7 %copy-start.20 = (s32[2560]{0:T(1024)S(1)}, s32[2560]{0:T(1024)}, u32[]{:S(2)}) copy-start(s32[2560]{0:T(1024)} %param.28) | copy-start | bytes 30724
  32.3 47.2 %all-to-all-start = ((bf16[128,16,256]{2,1,0:T(8,128)(2,1)}), bf16[128,16,256]{2,1,0:T(8,128)(2,1)S(1)}, u32[]{:S(2)}, u32[]{:S(2)}) async-start(bf16[128,16,256]{2,1,0:T(8,128)(2,1)} %bitcast.7), calls=%async_computation | async-start | bytes 2097152 | tf_op jit(solution)/shard_map/all_to_all | solution.py:406
  50.0 3.6 %collective-permute-start.10 = (bf16[2,1024,256]{2,1,0:T(8,128)(2,1)}, bf16[2,1024,256]{2,1,0:T(8,128)(2,1)S(1)}, u32[]{:S(2)}, u32[]{:S(2)}) collective-permute-start(bf16[2,1024,256]{2,1,0:T(8,128)(2,1)} %refs_9_.3), channel_id=1, source_target_pairs={{0,1},{1,0},{2,3},{3,2},{4,5},{5,4},{6,7},{7,6},{8,9},{9,8},{10,11... | collective-permute-start | bytes 3145736 | tf_op jit(solution)/shard_map/ppermute | solution.py:324
  50.5 3.0 %collective-permute-start.9 = (bf16[2,256,512]{2,1,0:T(8,128)(2,1)S(1)}, bf16[2,256,512]{2,1,0:T(8,128)(2,1)S(1)}, u32[]{:S(2)}, u32[]{:S(2)}) collective-permute-start(bf16[2,256,512]{2,1,0:T(8,128)(2,1)S(1)} %copy-done.9), channel_id=1, source_target_pairs={{0,1},{1,0},{2,3},{3,2},{4,5},{5,4},{6,7},{7,6},{8,9},{9,8},{10,11... | collective-permute-start | bytes 1572872 | tf_op jit(solution)/shard_map/ppermute | solution.py:324
  50.6 37.6 %collective-permute-start.12 = (bf16[2,256,512]{2,1,0:T(8,128)(2,1)S(1)}, bf16[2,256,512]{2,1,0:T(8,128)(2,1)S(1)}, u32[]{:S(2)}, u32[]{:S(2)}) collective-permute-start(bf16[2,256,512]{2,1,0:T(8,128)(2,1)S(1)} %copy-done.1), channel_id=1, source_target_pairs={{0,1},{1,0},{2,3},{3,2},{4,5},{5,4},{6,7},{7,6},{8,9},{9,8},{10,11... | collective-permute-start | bytes 1572872 | tf_op jit(solution)/shard_map/ppermute | solution.py:324
  53.5 0.8 copy-start.10
  53.5 1.2 copy-start.8
  62.2 27.0 %copy-start = (bf16[2,512,256]{2,1,0:T(8,128)(2,1)S(1)}, bf16[2,512,256]{2,1,0:T(8,128)(2,1)}, u32[]{:S(2)}) copy-start(bf16[2,512,256]{2,1,0:T(8,128)(2,1)} %refs_1_.6) | copy-start | bytes 1572868
  62.2 27.0 %copy-start.3 = (bf16[320,512]{1,0:T(8,128)(2,1)S(1)}, bf16[320,512]{1,0:T(8,128)(2,1)}, u32[]{:S(2)}) copy-start(bf16[320,512]{1,0:T(8,128)(2,1)} %get-tuple-element.63.refs_0_.refs_6_) | copy-start | bytes 983044
  62.2 27.0 %copy-start.7 = (bf16[512,512]{1,0:T(8,128)(2,1)S(1)}, bf16[512,512]{1,0:T(8,128)(2,1)}, u32[]{:S(2)}) copy-start(bf16[512,512]{1,0:T(8,128)(2,1)} %get-tuple-element.67.refs_2_) | copy-start | bytes 1572868
  79.4 9.8 %copy-start.4 = (f32[320,512]{1,0:T(8,128)S(1)}, f32[320,512]{1,0:T(8,128)}, u32[]{:S(2)}) copy-start(f32[320,512]{1,0:T(8,128)} %get-tuple-element.68.refs_3_) | copy-start | bytes 1966084
  85.3 3.9 %collective-permute-start.11 = (bf16[320,256]{1,0:T(8,128)(2,1)S(1)}, bf16[320,256]{1,0:T(8,128)(2,1)S(1)}, u32[]{:S(2)}, u32[]{:S(2)}) collective-permute-start(bf16[320,256]{1,0:T(8,128)(2,1)S(1)} %shard_map.205.refs_0_), channel_id=1, source_target_pairs={{0,1},{1,0},{2,3},{3,2},{4,5},{5,4},{6,7},{7,6},{8,9},{9,8},{10,11... | collective-permute-start | bytes 491528 | tf_op jit(solution)/shard_map/ppermute | solution.py:324
  91.9 35.8 %all-to-all-start.1 = ((bf16[128,16,256]{2,1,0:T(8,128)(2,1)}), bf16[128,16,256]{2,1,0:T(8,128)(2,1)S(1)}, u32[]{:S(2)}, u32[]{:S(2)}) async-start(bf16[128,16,256]{2,1,0:T(8,128)(2,1)} %bitcast.8), calls=%async_computation.1 | async-start | bytes 2097152 | tf_op jit(solution)/shard_map/all_to_all | solution.py:406
  105.9 31.4 %copy-start.2 = (bf16[320,512]{1,0:T(8,128)(2,1)S(1)}, bf16[320,512]{1,0:T(8,128)(2,1)}, u32[]{:S(2)}) copy-start(bf16[320,512]{1,0:T(8,128)(2,1)} %get-tuple-element.71.refs_0_.refs_6_) | copy-start | bytes 983044
  105.9 31.4 %copy-start.5 = (f32[320,512]{1,0:T(8,128)S(1)}, f32[320,512]{1,0:T(8,128)}, u32[]{:S(2)}) copy-start(f32[320,512]{1,0:T(8,128)} %get-tuple-element.74.refs_3_) | copy-start | bytes 1966084
  127.7 9.7 %copy-start.6 = (bf16[512,512]{1,0:T(8,128)(2,1)S(1)}, bf16[512,512]{1,0:T(8,128)(2,1)}, u32[]{:S(2)}) copy-start(bf16[512,512]{1,0:T(8,128)(2,1)} %get-tuple-element.73.refs_2_) | copy-start | bytes 1572868
  133.6 3.8 %collective-permute-start.13 = (bf16[320,256]{1,0:T(8,128)(2,1)S(1)}, bf16[320,256]{1,0:T(8,128)(2,1)S(1)}, u32[]{:S(2)}, u32[]{:S(2)}) collective-permute-start(bf16[320,256]{1,0:T(8,128)(2,1)S(1)} %shard_map.208.refs_0_), channel_id=1, source_target_pairs={{0,1},{1,0},{2,3},{3,2},{4,5},{5,4},{6,7},{7,6},{8,9},{9,8},{10,11... | collective-permute-start | bytes 491528 | tf_op jit(solution)/shard_map/ppermute | solution.py:324
where the time goes:
time: 139 us
  waiting for transfers between devices  51.2 us (37%)
  Pallas kernels  47.2 us (34%)
  starting transfers between devices  37.2 us (27%)
  local copies, waits for them, and re-layouts  2.96 us (2%)
    pallas_call x11, Pallas kernels, call(): pl.pallas_call(body, out_shape=[pltpu.HBM(shape, dtype) if pieces else ja...  47.2 us
    all_to_all x2, waiting for transfers between devices, shards(): lax.all_to_all(outgoing.reshape(bands, halo_slots, half), 'band', split_a...  39 us
    all_to_all x2, starting transfers between devices, shards(): lax.all_to_all(outgoing.reshape(bands, halo_slots, half), 'band', split_a...  24.1 us
    ppermute x13, starting transfers between devices, swap(): return lax.ppermute(values, 'tp', [(0, 1), (1, 0)])  11.8 us
    ppermute x13, waiting for transfers between devices, swap(): return lax.ppermute(values, 'tp', [(0, 1), (1, 0)])  7.62 us
    ppermute x1, waiting for transfers between devices, shards(): arrived = lax.ppermute(outgoing, ('band', 'tp'), pairs)  4.61 us
    unnamed x45, local copies, waits for them, and re-layouts  2.85 us
  transfers between devices with their start and end apart: 16, of which 9 were waited for; matrix products, arithmetic and copies ran while one was open for 0% of the time, Pallas kernels for 20%

commit v1 on v0

--- a/solution.py
+++ b/solution.py
@@ -2,6 +2,7 @@
 
 import jax
 import jax.numpy as jnp
+import numpy as np
 from jax import lax
 from jax.experimental import pallas as pl
 from jax.experimental.pallas import tpu as pltpu
@@ -394,8 +395,15 @@
         extra=[pltpu.VMEM((nodes, width), F32)],
     )
 
-    halo_row = halo_send.reshape(1, -1)
-    sender_row = edge_sender.reshape(1, -1)
+    order = (6, 5, 4, 3, 2, 1, 0)
+    bits = len(order)
+    members = np.arange(bands).reshape((2,) * bits).transpose(order).reshape(-1).tolist()
+    halo_row = halo_send.reshape((2,) * bits + (halo_slots,)).transpose(order + (bits,)).reshape(1, -1)
+    slot = edge_sender - nodes
+    place = slot & (halo_slots - 1)
+    for to, bit in enumerate(order):
+        place += ((slot // (halo_slots << (bits - 1 - bit))) & 1) * (halo_slots << (bits - 1 - to))
+    sender_row = jnp.where(slot < 0, edge_sender, place + nodes).reshape(1, -1)
     receiver_row = edge_receiver.reshape(1, -1)
     node_out = [((nodes, width), BF16, 1), ((bands * halo_slots, half), BF16, 4)]
 
@@ -404,7 +412,8 @@
             node_kernel, node_out, hidden, swap(hidden), *update, sender_w, halo_row
         )
         arrived = lax.all_to_all(
-            outgoing.reshape(bands, halo_slots, half), "band", split_axis=0, concat_axis=0, tiled=True
+            outgoing.reshape(bands, halo_slots, half), "band", split_axis=0, concat_axis=0,
+            axis_index_groups=[members], tiled=True
         ).reshape(bands * halo_slots, half)
         near, base, fold = call(
             edge_near_kernel, [((pieces * half, edge_rows), BF16, pieces)] + prepared, Far(latent),

time: 139 us -> 137 us (0.986)
  waiting for transfers between devices: 51.2 us -> 47.6 us
    all_to_all x2, waiting for transfers between devices: 39 us -> 35.5 us  [shards(): lax.all_to_all(outgoing.reshape(bands, halo_slots, half), 'band', split_a...]
    all_to_all x2, starting transfers between devices: 24.1 us -> 25.9 us  [shards(): lax.all_to_all(outgoing.reshape(bands, halo_slots, half), 'band', split_a...]
  transfers between devices with their start and end apart: 16 -> 16, of which waited for: 9 -> 9; matrix products, arithmetic and copies ran while one was open for 0% -> 0% of each run, Pallas kernels for 20% -> 21%
where the time goes in v1:
time: 137 us
  waiting for transfers between devices  47.6 us (35%)
  Pallas kernels  47.2 us (34%)
  starting transfers between devices  38.3 us (28%)
  local copies, waits for them, and re-layouts  3.06 us (2%)
    pallas_call x11, Pallas kernels, call(): pl.pallas_call(body, out_shape=[pltpu.HBM(shape, dtype) if pieces else ja...  47.2 us
    all_to_all x2, waiting for transfers between devices, shards(): lax.all_to_all(outgoing.reshape(bands, halo_slots, half), 'band', split_a...  35.5 us
    all_to_all x2, starting transfers between devices, shards(): lax.all_to_all(outgoing.reshape(bands, halo_slots, half), 'band', split_a...  25.9 us
    ppermute x13, starting transfers between devices, swap(): return lax.ppermute(values, 'tp', [(0, 1), (1, 0)])  11.1 us
    ppermute x13, waiting for transfers between devices, swap(): return lax.ppermute(values, 'tp', [(0, 1), (1, 0)])  7.47 us
    ppermute x1, waiting for transfers between devices, shards(): arrived = lax.ppermute(outgoing, ('band', 'tp'), pairs)  4.61 us
    unnamed x45, local copies, waits for them, and re-layouts  2.85 us
  transfers between devices with their start and end apart: 16, of which 9 were waited for; matrix products, arithmetic and copies ran while one was open for 0% of the time, Pallas kernels for 21%

profile of v1, /device:TPU:1, one launch (start us, length us, event | category | flops | bytes accessed | tf_op | source)
XLA Modules:
  0.0 136.6 jit_solution(9722588110180398028)
XLA Ops:
  0.0 3.2 %collective-permute-start.1 = (bf16[256,512]{1,0:T(8,128)(2,1)}, bf16[256,512]{1,0:T(8,128)(2,1)S(1)}, u32[]{:S(2)}, u32[]{:S(2)}) collective-permute-start(bf16[256,512]{1,0:T(8,128)(2,1)} %refs_2_.4), channel_id=1, source_target_pairs={{0,1},{1,0},{2,3},{3,2},{4,5},{5,4},{6,7},{7,6},{8,9},{9,8},{10,11... | collective-permute-start | bytes 786440 | tf_op jit(solution)/shard_map/ppermute | solution.py:325
  3.2 0.0 collective-permute-start.2
  3.2 0.5 collective-permute-start
  3.8 2.1 %shard_map.199 = (bf16[256,1024]{1,0:T(8,128)(2,1)S(1)}, bf16[474,1024]{1,0:T(8,128)(2,1)S(1)}, bf16[256,512]{1,0:T(8,128)(2,1)S(1)}, bf16[512,256]{1,0:T(8,128)(2,1)S(1)}) custom-call(bf16[474,1024]{1,0:T(8,128)(2,1)} %bitcast.12, bf16[474,256]{1,0:T(8,128)(2,1)} %refs_1_.3, bf16[256,512]{1,0:T(8,128)(2,1)} %refs_2_.4, bf16[512,256]{1,0:T(8,128)(2,1)} %refs_3_.4), custom_call_target="tpu_custom_call" | custom-call | tf_op jit(solution)/shard_map/pallas_call | solution.py:166
  5.8 0.0 collective-permute-done.refs_2_
  5.8 0.0 collective-permute-done.1.refs_4_
  5.8 0.0 collective-permute-done.2.refs_6_
  5.8 0.0 copy-start.11
  5.9 0.0 copy-start.15
  5.9 0.0 copy-start.16
  5.9 0.0 copy-start.13
  5.9 3.9 %shard_map.200 = (bf16[512,1024]{1,0:T(8,128)(2,1)S(1)}, bf16[512,1024]{1,0:T(8,128)(2,1)S(1)}) custom-call(bf16[474,1024]{1,0:T(8,128)(2,1)S(1)} %get-tuple-element.40.refs_0_, bf16[256,1024]{1,0:T(8,128)(2,1)S(1)} %get-tuple-element.41.refs_1_, bf16[474,256]{1,0:T(8,128)(2,1)S(1)} %collective-permute-done.refs_2_, ...), custom_call_target="tpu_custom_call" | custom-call | tf_op jit(solution)/shard_map/pallas_call | solution.py:166
  9.8 1.3 collective-permute-start.6
  11.1 0.5 collective-permute-start.5
  11.6 0.1 collective-permute-start.3
  11.7 0.4 collective-permute-start.4
  12.2 0.1 collective-permute-start.7
  12.3 1.3 collective-permute-done.3.refs_2_
  13.6 0.4 collective-permute-done.4.refs_7_
  13.9 0.0 collective-permute-done.5.refs_9_
  13.9 0.3 copy-done.17
  14.3 0.4 copy-done.18
  14.6 0.8 copy-done.12
  15.4 5.3 %shard_map.201 = (bf16[512,320]{1,0:T(8,128)(2,1)S(1)}, f32[320,512]{1,0:T(8,128)S(1)}, f32[320,512]{1,0:T(8,128)}, bf16[512,512]{1,0:T(8,128)(2,1)}) custom-call(bf16[320,512]{1,0:T(8,128)(2,1)} %refs_8_.2, bf16[512,256]{1,0:T(8,128)(2,1)} %refs_1_.4, bf16[512,256]{1,0:T(8,128)(2,1)} %copy-done.17, s32[3,1024]{1,0:T(4,128)} %refs_3_.5, s32[3,1024]{1,0:T(4,128)} %refs_2_.5, ...), custom_call_target="tpu_custom_call" | custom-call | tf_op jit(solution)/shard_map/pallas_call | solution.py:166
  20.7 0.0 collective-permute-done.7.refs_7_
  20.7 0.0 copy-start.14
  20.7 4.6 %collective-permute-done.6.refs_3_ = bf16[512,1024]{1,0:T(8,128)(2,1)S(1)} collective-permute-done((bf16[512,1024]{1,0:T(8,128)(2,1)S(1)}, bf16[512,1024]{1,0:T(8,128)(2,1)S(1)}, u32[]{:S(2)}, u32[]{:S(2)}) %collective-permute-start.6) | collective-permute-done | bytes 1048608 | tf_op jit(solution)/shard_map/ppermute | solution.py:372
  25.4 2.3 %shard_map.202 = (bf16[320,512]{1,0:T(8,128)(2,1)S(1)}, bf16[512,512]{1,0:T(8,128)(2,1)S(1)}, f32[320,512]{1,0:T(8,128)S(1)}, bf16[256,512]{1,0:T(8,128)(2,1)S(1...) custom-call(bf16[512,320]{1,0:T(8,128)(2,1)S(1)} %get-tuple-element.49.refs_0_, ...), custom_call_target="tpu_custom_call" | custom-call | tf_op jit(solution)/shard_map/pallas_call | solution.py:166
  27.7 0.3 collective-permute-start.8
  28.0 0.1 copy.23
  28.1 0.1 copy.24
  28.1 0.1 reshape.25.refs_8_
  28.2 1.3 collective-permute-done.8.refs_1_
  29.6 2.7 %shard_map.203 = (bf16[320,512]{1,0:T(8,128)(2,1)}, bf16[2048,256]{1,0:T(8,128)(2,1)}) custom-call(bf16[320,512]{1,0:T(8,128)(2,1)S(1)} %get-tuple-element.55.refs_0_, bf16[320,512]{1,0:T(8,128)(2,1)S(1)} %collective-permute-done.8.refs_1_, bf16[512,512]{1,0:T(8,128)(2,1)S(1)} %get-tuple-element.56.refs_2_, f32[320,512]{1,0:T(8,128)S(1)} %get-tuple-element.57.refs_3_, ...), custom_call_target="tpu_custom_call" | custom-call | tf_op jit(solution)/shard_map/pallas_call | solution.py:166
  32.2 0.0 copy-start.9
  32.3 0.0 copy-start.1
  32.3 0.0 copy-start.19
  32.3 0.0 copy-start.20
  32.3 17.7 %all-to-all-start = ((bf16[128,16,256]{2,1,0:T(8,128)(2,1)}), bf16[128,16,256]{2,1,0:T(8,128)(2,1)S(1)}, u32[]{:S(2)}, u32[]{:S(2)}) async-start(bf16[128,16,256]{2,1,0:T(8,128)(2,1)} %bitcast.10), calls=%async_computation | async-start | bytes 2097152 | tf_op jit(solution)/shard_map/all_to_all | solution.py:414
  50.0 0.5 collective-permute-start.10
  50.5 0.1 collective-permute-start.9
  50.6 0.4 collective-permute-start.12
  51.0 0.1 fusion.11
  51.1 2.4 %collective-permute-done.9.refs_8_ = bf16[2,256,512]{2,1,0:T(8,128)(2,1)S(1)} collective-permute-done((bf16[2,256,512]{2,1,0:T(8,128)(2,1)S(1)}, bf16[2,256,512]{2,1,0:T(8,128)(2,1)S(1)}, u32[]{:S(2)}, u32[]{:S(2)}) %collective-permute-start.9) | collective-permute-done | bytes 524320 | tf_op jit(solution)/shard_map/ppermute | solution.py:325
  53.5 0.0 collective-permute-done.10.refs_10_
  53.5 0.8 copy-done.10
  54.3 0.4 copy-done.8
  54.7 7.5 %shard_map.204 = (bf16[1280,512]{1,0:T(8,128)(2,1)}, f32[320,512]{1,0:T(8,128)}, bf16[512,512]{1,0:T(8,128)(2,1)}) custom-call(bf16[320,512]{1,0:T(8,128)(2,1)} %get-tuple-element.63.refs_0_.refs_6_, bf16[2,512,256]{2,1,0:T(8,128)(2,1)} %refs_1_.6, bf16[2,512,256]{2,1,0:T(8,128)(2,1)} %refs_2_.7, bf16[2,512,256]{2,1,0:T(8,128)(2,1)} %refs_3_.7, ...), custom_call_target="tpu_custom_call" | custom-call | tf_op jit(solution)/shard_map/pallas_call | solution.py:166
  62.2 0.0 copy-start
  62.3 0.0 copy-start.3
  62.3 15.7 %all-to-all-done = bf16[128,16,256]{2,1,0:T(8,128)(2,1)S(1)} async-done(((bf16[128,16,256]{2,1,0:T(8,128)(2,1)}), bf16[128,16,256]{2,1,0:T(8,128)(2,1)S(1)}, u32[]{:S(2)}, u32[]{:S(2)}) %all-to-all-start) | async-done | bytes 1048608 | tf_op jit(solution)/shard_map/all_to_all | solution.py:414
  78.0 5.9 %shard_map.205.refs_0_ = bf16[320,256]{1,0:T(8,128)(2,1)S(1)} custom-call(bf16[2048,256]{1,0:T(8,128)(2,1)S(1)} %bitcast.8, bf16[1280,512]{1,0:T(8,128)(2,1)} %get-tuple-element.66.refs_1_, s32[1,2560]{1,0:T(1,128)S(1)} %reshape.28.refs_5_.refs_2_, s32[1,2560]{1,0:T(1,128)S(1)} %reshape.29.refs_6_.refs_3_), custom_call_target="tpu_custom_call" | custom-call | tf_op jit(solution)/shard_map/pallas_call | solution.py:166
  83.9 2.2 %collective-permute-start.11 = (bf16[320,256]{1,0:T(8,128)(2,1)S(1)}, bf16[320,256]{1,0:T(8,128)(2,1)S(1)}, u32[]{:S(2)}, u32[]{:S(2)}) collective-permute-start(bf16[320,256]{1,0:T(8,128)(2,1)S(1)} %shard_map.205.refs_0_), channel_id=1, source_target_pairs={{0,1},{1,0},{2,3},{3,2},{4,5},{5,4},{6,7},{7,6},{8,9},{9,8},{10,11... | collective-permute-start | bytes 491528 | tf_op jit(solution)/shard_map/ppermute | solution.py:325
  86.1 0.0 collective-permute-done.12.refs_5_
  86.1 1.0 collective-permute-done.11.refs_1_
  87.1 2.6 %shard_map.206 = (bf16[320,512]{1,0:T(8,128)(2,1)}, bf16[2048,256]{1,0:T(8,128)(2,1)}) custom-call(bf16[320,256]{1,0:T(8,128)(2,1)S(1)} %shard_map.205.refs_0_, bf16[320,256]{1,0:T(8,128)(2,1)S(1)} %collective-permute-done.11.refs_1_, bf16[512,512]{1,0:T(8,128)(2,1)S(1)} %copy-done.7, f32[320,512]{1,0:T(8,128)S(1)} %copy-done.4, ...), custom_call_target="tpu_custom_call" | custom-call | tf_op jit(solution)/shard_map/pallas_call | solution.py:166
  89.7 8.2 %all-to-all-start.1 = ((bf16[128,16,256]{2,1,0:T(8,128)(2,1)}), bf16[128,16,256]{2,1,0:T(8,128)(2,1)S(1)}, u32[]{:S(2)}, u32[]{:S(2)}) async-start(bf16[128,16,256]{2,1,0:T(8,128)(2,1)} %bitcast.11), calls=%async_computation.1 | async-start | bytes 2097152 | tf_op jit(solution)/shard_map/all_to_all | solution.py:414
  98.0 7.5 %shard_map.207 = (bf16[1280,512]{1,0:T(8,128)(2,1)}, f32[320,512]{1,0:T(8,128)}, bf16[512,512]{1,0:T(8,128)(2,1)}) custom-call(bf16[320,512]{1,0:T(8,128)(2,1)} %get-tuple-element.71.refs_0_.refs_6_, bf16[2,512,256]{2,1,0:T(8,128)(2,1)} %refs_1_.6, bf16[2,512,256]{2,1,0:T(8,128)(2,1)} %refs_2_.7, bf16[2,512,256]{2,1,0:T(8,128)(2,1)} %refs_3_.7, ...), custom_call_target="tpu_custom_call" | custom-call | tf_op jit(solution)/shard_map/pallas_call | solution.py:166
  105.5 0.0 copy-start.2
  105.5 19.7 %all-to-all-done.1 = bf16[128,16,256]{2,1,0:T(8,128)(2,1)S(1)} async-done(((bf16[128,16,256]{2,1,0:T(8,128)(2,1)}), bf16[128,16,256]{2,1,0:T(8,128)(2,1)S(1)}, u32[]{:S(2)}, u32[]{:S(2)}) %all-to-all-start.1) | async-done | bytes 1048608 | tf_op jit(solution)/shard_map/all_to_all | solution.py:414
  125.3 5.9 %shard_map.208.refs_0_ = bf16[320,256]{1,0:T(8,128)(2,1)S(1)} custom-call(bf16[2048,256]{1,0:T(8,128)(2,1)S(1)} %bitcast.9, bf16[1280,512]{1,0:T(8,128)(2,1)} %get-tuple-element.72.refs_1_, s32[1,2560]{1,0:T(1,128)S(1)} %reshape.28.refs_5_.refs_2_, s32[1,2560]{1,0:T(1,128)S(1)} %reshape.29.refs_6_.refs_3_), custom_call_target="tpu_custom_call" | custom-call | tf_op jit(solution)/shard_map/pallas_call | solution.py:166
  131.1 2.7 %collective-permute-start.13 = (bf16[320,256]{1,0:T(8,128)(2,1)S(1)}, bf16[320,256]{1,0:T(8,128)(2,1)S(1)}, u32[]{:S(2)}, u32[]{:S(2)}) collective-permute-start(bf16[320,256]{1,0:T(8,128)(2,1)S(1)} %shard_map.208.refs_0_), channel_id=1, source_target_pairs={{0,1},{1,0},{2,3},{3,2},{4,5},{5,4},{6,7},{7,6},{8,9},{9,8},{10,11... | collective-permute-start | bytes 491528 | tf_op jit(solution)/shard_map/ppermute | solution.py:325
  133.8 1.0 collective-permute-done.13.refs_1_
  134.9 1.5 %shard_map.209 = bf16[320,512]{1,0:T(8,128)(2,1)} custom-call(bf16[320,256]{1,0:T(8,128)(2,1)S(1)} %shard_map.208.refs_0_, bf16[320,256]{1,0:T(8,128)(2,1)S(1)} %collective-permute-done.13.refs_1_, bf16[512,512]{1,0:T(8,128)(2,1)S(1)} %copy-done.6, f32[320,512]{1,0:T(8,128)S(1)} %copy-done.5, bf16[2,256,512]{2,1,0:T(8,128)(2,1)S(1)} %copy-done.1, ...), custom_call_target="tpu_custom_call" | custom-call | tf_op jit(solution)/shard_map/pallas_call | solution.py:166
  (29 shorter events, 0.1 us)
Async XLA Ops:
  0.0 5.8 %collective-permute-start.1 = (bf16[256,512]{1,0:T(8,128)(2,1)}, bf16[256,512]{1,0:T(8,128)(2,1)S(1)}, u32[]{:S(2)}, u32[]{:S(2)}) collective-permute-start(bf16[256,512]{1,0:T(8,128)(2,1)} %refs_2_.4), channel_id=1, source_target_pairs={{0,1},{1,0},{2,3},{3,2},{4,5},{5,4},{6,7},{7,6},{8,9},{9,8},{10,11... | collective-permute-start | bytes 786440 | tf_op jit(solution)/shard_map/ppermute | solution.py:325
  3.2 2.6 %collective-permute-start.2 = (bf16[512,256]{1,0:T(8,128)(2,1)}, bf16[512,256]{1,0:T(8,128)(2,1)S(1)}, u32[]{:S(2)}, u32[]{:S(2)}) collective-permute-start(bf16[512,256]{1,0:T(8,128)(2,1)} %refs_3_.4), channel_id=1, source_target_pairs={{0,1},{1,0},{2,3},{3,2},{4,5},{5,4},{6,7},{7,6},{8,9},{9,8},{10,11... | collective-permute-start | bytes 786440 | tf_op jit(solution)/shard_map/ppermute | solution.py:325
  3.2 2.6 %collective-permute-start = (bf16[474,256]{1,0:T(8,128)(2,1)}, bf16[474,256]{1,0:T(8,128)(2,1)S(1)}, u32[]{:S(2)}, u32[]{:S(2)}) collective-permute-start(bf16[474,256]{1,0:T(8,128)(2,1)} %refs_1_.3), channel_id=1, source_target_pairs={{0,1},{1,0},{2,3},{3,2},{4,5},{5,4},{6,7},{7,6},{8,9},{9,8},{10,11... | collective-permute-start | bytes 728072 | tf_op jit(solution)/shard_map/ppermute | solution.py:325
  5.8 5.3 %copy-start.11 = (bf16[1024,256]{1,0:T(8,128)(2,1)S(1)}, bf16[1024,256]{1,0:T(8,128)(2,1)}, u32[]{:S(2)}) copy-start(bf16[1024,256]{1,0:T(8,128)(2,1)} %refs_8_.1) | copy-start | bytes 1572868
  5.9 5.8 %copy-start.15 = (bf16[512,256]{1,0:T(8,128)(2,1)S(1)}, bf16[512,256]{1,0:T(8,128)(2,1)}, u32[]{:S(2)}) copy-start(bf16[512,256]{1,0:T(8,128)(2,1)} %refs_1_.4) | copy-start | bytes 786436
  5.9 5.9 %copy-start.16 = (bf16[256,512]{1,0:T(8,128)(2,1)S(1)}, bf16[256,512]{1,0:T(8,128)(2,1)}, u32[]{:S(2)}) copy-start(bf16[256,512]{1,0:T(8,128)(2,1)} %refs_6_) | copy-start | bytes 786436
  5.9 6.3 %copy-start.13 = (bf16[256,512]{1,0:T(8,128)(2,1)S(1)}, bf16[256,512]{1,0:T(8,128)(2,1)}, u32[]{:S(2)}) copy-start(bf16[256,512]{1,0:T(8,128)(2,1)} %refs_6_.1) | copy-start | bytes 786436
  9.8 15.5 %collective-permute-start.6 = (bf16[512,1024]{1,0:T(8,128)(2,1)S(1)}, bf16[512,1024]{1,0:T(8,128)(2,1)S(1)}, u32[]{:S(2)}, u32[]{:S(2)}) collective-permute-start(bf16[512,1024]{1,0:T(8,128)(2,1)S(1)} %get-tuple-element.51), channel_id=1, source_target_pairs={{0,2},{2,4},{4,6},{6,8},{8,10},{10,12},{12,14},{14,16},{16,18},{18... | collective-permute-start | bytes 3145736 | tf_op jit(solution)/shard_map/ppermute | solution.py:372
  11.1 2.8 %collective-permute-start.5 = (bf16[1024,256]{1,0:T(8,128)(2,1)S(1)}, bf16[1024,256]{1,0:T(8,128)(2,1)S(1)}, u32[]{:S(2)}, u32[]{:S(2)}) collective-permute-start(bf16[1024,256]{1,0:T(8,128)(2,1)S(1)} %copy-done.11), channel_id=1, source_target_pairs={{0,1},{1,0},{2,3},{3,2},{4,5},{5,4},{6,7},{7,6},{8,9},{9,8},{10,11... | collective-permute-start | bytes 1572872 | tf_op jit(solution)/shard_map/ppermute | solution.py:325
  11.6 1.9 %collective-permute-start.3 = (bf16[512,256]{1,0:T(8,128)(2,1)S(1)}, bf16[512,256]{1,0:T(8,128)(2,1)S(1)}, u32[]{:S(2)}, u32[]{:S(2)}) collective-permute-start(bf16[512,256]{1,0:T(8,128)(2,1)S(1)} %copy-done.15), channel_id=1, source_target_pairs={{0,1},{1,0},{2,3},{3,2},{4,5},{5,4},{6,7},{7,6},{8,9},{9,8},{10,11... | collective-permute-start | bytes 786440 | tf_op jit(solution)/shard_map/ppermute | solution.py:325
  11.7 2.2 %collective-permute-start.4 = (bf16[256,512]{1,0:T(8,128)(2,1)S(1)}, bf16[256,512]{1,0:T(8,128)(2,1)S(1)}, u32[]{:S(2)}, u32[]{:S(2)}) collective-permute-start(bf16[256,512]{1,0:T(8,128)(2,1)S(1)} %copy-done.16), channel_id=1, source_target_pairs={{0,1},{1,0},{2,3},{3,2},{4,5},{5,4},{6,7},{7,6},{8,9},{9,8},{10,11... | collective-permute-start | bytes 786440 | tf_op jit(solution)/shard_map/ppermute | solution.py:325
  12.2 8.6 %collective-permute-start.7 = (bf16[256,512]{1,0:T(8,128)(2,1)S(1)}, bf16[256,512]{1,0:T(8,128)(2,1)S(1)}, u32[]{:S(2)}, u32[]{:S(2)}) collective-permute-start(bf16[256,512]{1,0:T(8,128)(2,1)S(1)} %copy-done.13), channel_id=1, source_target_pairs={{0,1},{1,0},{2,3},{3,2},{4,5},{5,4},{6,7},{7,6},{8,9},{9,8},{10,11... | collective-permute-start | bytes 786440 | tf_op jit(solution)/shard_map/ppermute | solution.py:325
  13.5 0.7 copy-start.17
  13.9 0.7 copy-start.18
  14.6 0.8 copy-start.12
  20.7 4.6 %copy-start.14 = (bf16[256,512]{1,0:T(8,128)(2,1)}, bf16[256,512]{1,0:T(8,128)(2,1)S(1)}, u32[]{:S(2)}) copy-start(bf16[256,512]{1,0:T(8,128)(2,1)S(1)} %collective-permute-done.7.refs_7_) | copy-start | bytes 786436
  25.4 2.6 %copy-start.21 = (s32[128,16]{0,1:T(8,128)S(1)}, s32[128,16]{0,1:T(8,128)}, u32[]{:S(2)}) copy-start(s32[128,16]{0,1:T(8,128)} %param.26) | copy-start | bytes 24580
  27.7 1.9 %collective-permute-start.8 = (bf16[320,512]{1,0:T(8,128)(2,1)S(1)}, bf16[320,512]{1,0:T(8,128)(2,1)S(1)}, u32[]{:S(2)}, u32[]{:S(2)}) collective-permute-start(bf16[320,512]{1,0:T(8,128)(2,1)S(1)} %get-tuple-element.55.refs_0_), channel_id=1, source_target_pairs={{0,1},{1,0},{2,3},{3,2},{4,5},{5,4},{6,7},{7,6},{8,9},{9,8},{10,11... | collective-permute-start | bytes 983048 | tf_op jit(solution)/shard_map/ppermute | solution.py:325
  32.2 18.3 %copy-start.9 = (bf16[2,256,512]{2,1,0:T(8,128)(2,1)S(1)}, bf16[2,256,512]{2,1,0:T(8,128)(2,1)}, u32[]{:S(2)}) copy-start(bf16[2,256,512]{2,1,0:T(8,128)(2,1)} %refs_7_.5) | copy-start | bytes 1572868
  32.3 18.4 %copy-start.1 = (bf16[2,256,512]{2,1,0:T(8,128)(2,1)S(1)}, bf16[2,256,512]{2,1,0:T(8,128)(2,1)}, u32[]{:S(2)}) copy-start(bf16[2,256,512]{2,1,0:T(8,128)(2,1)} %refs_4_.7) | copy-start | bytes 1572868
  32.3 18.7 %copy-start.19 = (s32[2560]{0:T(1024)S(1)}, s32[2560]{0:T(1024)}, u32[]{:S(2)}) copy-start(s32[2560]{0:T(1024)} %param.27) | copy-start | bytes 30724
  32.3 18.8 %copy-start.20 = (s32[2560]{0:T(1024)S(1)}, s32[2560]{0:T(1024)}, u32[]{:S(2)}) copy-start(s32[2560]{0:T(1024)} %param.28) | copy-start | bytes 30724
  32.3 45.7 %all-to-all-start = ((bf16[128,16,256]{2,1,0:T(8,128)(2,1)}), bf16[128,16,256]{2,1,0:T(8,128)(2,1)S(1)}, u32[]{:S(2)}, u32[]{:S(2)}) async-start(bf16[128,16,256]{2,1,0:T(8,128)(2,1)} %bitcast.10), calls=%async_computation | async-start | bytes 2097152 | tf_op jit(solution)/shard_map/all_to_all | solution.py:414
  50.0 3.6 %collective-permute-start.10 = (bf16[2,1024,256]{2,1,0:T(8,128)(2,1)}, bf16[2,1024,256]{2,1,0:T(8,128)(2,1)S(1)}, u32[]{:S(2)}, u32[]{:S(2)}) collective-permute-start(bf16[2,1024,256]{2,1,0:T(8,128)(2,1)} %refs_9_.3), channel_id=1, source_target_pairs={{0,1},{1,0},{2,3},{3,2},{4,5},{5,4},{6,7},{7,6},{8,9},{9,8},{10,11... | collective-permute-start | bytes 3145736 | tf_op jit(solution)/shard_map/ppermute | solution.py:325
  50.5 3.0 %collective-permute-start.9 = (bf16[2,256,512]{2,1,0:T(8,128)(2,1)S(1)}, bf16[2,256,512]{2,1,0:T(8,128)(2,1)S(1)}, u32[]{:S(2)}, u32[]{:S(2)}) collective-permute-start(bf16[2,256,512]{2,1,0:T(8,128)(2,1)S(1)} %copy-done.9), channel_id=1, source_target_pairs={{0,1},{1,0},{2,3},{3,2},{4,5},{5,4},{6,7},{7,6},{8,9},{9,8},{10,11... | collective-permute-start | bytes 1572872 | tf_op jit(solution)/shard_map/ppermute | solution.py:325
  50.6 35.4 %collective-permute-start.12 = (bf16[2,256,512]{2,1,0:T(8,128)(2,1)S(1)}, bf16[2,256,512]{2,1,0:T(8,128)(2,1)S(1)}, u32[]{:S(2)}, u32[]{:S(2)}) collective-permute-start(bf16[2,256,512]{2,1,0:T(8,128)(2,1)S(1)} %copy-done.1), channel_id=1, source_target_pairs={{0,1},{1,0},{2,3},{3,2},{4,5},{5,4},{6,7},{7,6},{8,9},{9,8},{10,11... | collective-permute-start | bytes 1572872 | tf_op jit(solution)/shard_map/ppermute | solution.py:325
  53.5 0.8 copy-start.10
  53.5 1.2 copy-start.8
  62.2 24.8 %copy-start = (bf16[2,512,256]{2,1,0:T(8,128)(2,1)S(1)}, bf16[2,512,256]{2,1,0:T(8,128)(2,1)}, u32[]{:S(2)}) copy-start(bf16[2,512,256]{2,1,0:T(8,128)(2,1)} %refs_1_.6) | copy-start | bytes 1572868
  62.3 24.8 %copy-start.3 = (bf16[320,512]{1,0:T(8,128)(2,1)S(1)}, bf16[320,512]{1,0:T(8,128)(2,1)}, u32[]{:S(2)}) copy-start(bf16[320,512]{1,0:T(8,128)(2,1)} %get-tuple-element.63.refs_0_.refs_6_) | copy-start | bytes 983044
  62.3 24.8 %copy-start.7 = (bf16[512,512]{1,0:T(8,128)(2,1)S(1)}, bf16[512,512]{1,0:T(8,128)(2,1)}, u32[]{:S(2)}) copy-start(bf16[512,512]{1,0:T(8,128)(2,1)} %get-tuple-element.67.refs_2_) | copy-start | bytes 1572868
  78.0 9.1 %copy-start.4 = (f32[320,512]{1,0:T(8,128)S(1)}, f32[320,512]{1,0:T(8,128)}, u32[]{:S(2)}) copy-start(f32[320,512]{1,0:T(8,128)} %get-tuple-element.68.refs_3_) | copy-start | bytes 1966084
  83.9 3.2 %collective-permute-start.11 = (bf16[320,256]{1,0:T(8,128)(2,1)S(1)}, bf16[320,256]{1,0:T(8,128)(2,1)S(1)}, u32[]{:S(2)}, u32[]{:S(2)}) collective-permute-start(bf16[320,256]{1,0:T(8,128)(2,1)S(1)} %shard_map.205.refs_0_), channel_id=1, source_target_pairs={{0,1},{1,0},{2,3},{3,2},{4,5},{5,4},{6,7},{7,6},{8,9},{9,8},{10,11... | collective-permute-start | bytes 491528 | tf_op jit(solution)/shard_map/ppermute | solution.py:325
  89.7 35.5 %all-to-all-start.1 = ((bf16[128,16,256]{2,1,0:T(8,128)(2,1)}), bf16[128,16,256]{2,1,0:T(8,128)(2,1)S(1)}, u32[]{:S(2)}, u32[]{:S(2)}) async-start(bf16[128,16,256]{2,1,0:T(8,128)(2,1)} %bitcast.11), calls=%async_computation.1 | async-start | bytes 2097152 | tf_op jit(solution)/shard_map/all_to_all | solution.py:414
  105.5 29.4 %copy-start.2 = (bf16[320,512]{1,0:T(8,128)(2,1)S(1)}, bf16[320,512]{1,0:T(8,128)(2,1)}, u32[]{:S(2)}) copy-start(bf16[320,512]{1,0:T(8,128)(2,1)} %get-tuple-element.71.refs_0_.refs_6_) | copy-start | bytes 983044
  105.5 29.3 %copy-start.5 = (f32[320,512]{1,0:T(8,128)S(1)}, f32[320,512]{1,0:T(8,128)}, u32[]{:S(2)}) copy-start(f32[320,512]{1,0:T(8,128)} %get-tuple-element.74.refs_3_) | copy-start | bytes 1966084
  125.3 9.6 %copy-start.6 = (bf16[512,512]{1,0:T(8,128)(2,1)S(1)}, bf16[512,512]{1,0:T(8,128)(2,1)}, u32[]{:S(2)}) copy-start(bf16[512,512]{1,0:T(8,128)(2,1)} %get-tuple-element.73.refs_2_) | copy-start | bytes 1572868
  131.1 3.7 %collective-permute-start.13 = (bf16[320,256]{1,0:T(8,128)(2,1)S(1)}, bf16[320,256]{1,0:T(8,128)(2,1)S(1)}, u32[]{:S(2)}, u32[]{:S(2)}) collective-permute-start(bf16[320,256]{1,0:T(8,128)(2,1)S(1)} %shard_map.208.refs_0_), channel_id=1, source_target_pairs={{0,1},{1,0},{2,3},{3,2},{4,5},{5,4},{6,7},{7,6},{8,9},{9,8},{10,11... | collective-permute-start | bytes 491528 | tf_op jit(solution)/shard_map/ppermute | solution.py:325

commit v2 on v1

--- a/solution.py
+++ b/solution.py
@@ -354,8 +354,8 @@
     half = encode_sender.shape[1]
     bands, halo_slots = halo_send.shape
     layers = layer_sender.shape[0]
-    pieces = 5
-    block = 512
+    pieces = 1
+    block = 1024
     edge_rows = edge_latent.shape[0] // pieces
 
     own, x, out_own, sender_own = call(

time: 137 us -> 133 us (0.971)
  Pallas kernels: 47.2 us -> 42 us
  waiting for transfers between devices: 47.6 us -> 49 us
    pallas_call x11, Pallas kernels: 47.2 us -> 42 us  [call(): pl.pallas_call(body, out_shape=[pltpu.HBM(shape, dtype) if pieces else ja...]
    all_to_all x2, waiting for transfers between devices: 35.5 us -> 37.1 us  [shards(): lax.all_to_all(outgoing.reshape(bands, halo_slots, half), 'band', split_a...]
  transfers between devices with their start and end apart: 16 -> 16, of which waited for: 9 -> 9; matrix products, arithmetic and copies ran while one was open for 0% -> 0% of each run, Pallas kernels for 21% -> 19%
where the time goes in v2:
time: 133 us
  waiting for transfers between devices  49 us (37%)
  Pallas kernels  42 us (32%)
  starting transfers between devices  38.4 us (29%)
  local copies, waits for them, and re-layouts  3.06 us (2%)
    pallas_call x11, Pallas kernels, call(): pl.pallas_call(body, out_shape=[pltpu.HBM(shape, dtype) if pieces else ja...  42 us
    all_to_all x2, waiting for transfers between devices, shards(): lax.all_to_all(outgoing.reshape(bands, halo_slots, half), 'band', split_a...  37.1 us
    all_to_all x2, starting transfers between devices, shards(): lax.all_to_all(outgoing.reshape(bands, halo_slots, half), 'band', split_a...  25.9 us
    ppermute x13, starting transfers between devices, swap(): return lax.ppermute(values, 'tp', [(0, 1), (1, 0)])  11.2 us
    ppermute x13, waiting for transfers between devices, swap(): return lax.ppermute(values, 'tp', [(0, 1), (1, 0)])  7.47 us
    ppermute x1, waiting for transfers between devices, shards(): arrived = lax.ppermute(outgoing, ('band', 'tp'), pairs)  4.46 us
    unnamed x45, local copies, waits for them, and re-layouts  2.85 us
  transfers between devices with their start and end apart: 16, of which 9 were waited for; matrix products, arithmetic and copies ran while one was open for 0% of the time, Pallas kernels for 19%

profile of v2, /device:TPU:1, one launch (start us, length us, event | category | flops | bytes accessed | tf_op | source)
XLA Modules:
  0.0 133.1 jit_solution(11816182045265202379)
XLA Ops:
  0.0 3.2 %collective-permute-start.1 = (bf16[256,512]{1,0:T(8,128)(2,1)}, bf16[256,512]{1,0:T(8,128)(2,1)S(1)}, u32[]{:S(2)}, u32[]{:S(2)}) collective-permute-start(bf16[256,512]{1,0:T(8,128)(2,1)} %refs_2_.4), channel_id=1, source_target_pairs={{0,1},{1,0},{2,3},{3,2},{4,5},{5,4},{6,7},{7,6},{8,9},{9,8},{10,11... | collective-permute-start | bytes 786440 | tf_op jit(solution)/shard_map/ppermute | solution.py:325
  3.2 0.0 collective-permute-start.2
  3.2 0.5 collective-permute-start
  3.8 1.8 %shard_map.199 = (bf16[256,1024]{1,0:T(8,128)(2,1)S(1)}, bf16[474,1024]{1,0:T(8,128)(2,1)S(1)}, bf16[256,512]{1,0:T(8,128)(2,1)S(1)}, bf16[512,256]{1,0:T(8,128)(2,1)S(1)}) custom-call(bf16[474,1024]{1,0:T(8,128)(2,1)} %bitcast.12, bf16[474,256]{1,0:T(8,128)(2,1)} %refs_1_.3, bf16[256,512]{1,0:T(8,128)(2,1)} %refs_2_.4, bf16[512,256]{1,0:T(8,128)(2,1)} %refs_3_.4), custom_call_target="tpu_custom_call" | custom-call | tf_op jit(solution)/shard_map/pallas_call | solution.py:166
  5.5 0.0 collective-permute-done.refs_2_
  5.5 0.0 collective-permute-done.1.refs_4_
  5.6 0.0 collective-permute-done.2.refs_6_
  5.6 0.0 copy-start.11
  5.6 0.0 copy-start.15
  5.6 0.0 copy-start.16
  5.6 0.0 copy-start.13
  5.6 3.3 %shard_map.200 = (bf16[512,1024]{1,0:T(8,128)(2,1)S(1)}, bf16[512,1024]{1,0:T(8,128)(2,1)S(1)}) custom-call(bf16[474,1024]{1,0:T(8,128)(2,1)S(1)} %get-tuple-element.40.refs_0_, bf16[256,1024]{1,0:T(8,128)(2,1)S(1)} %get-tuple-element.41.refs_1_, bf16[474,256]{1,0:T(8,128)(2,1)S(1)} %collective-permute-done.refs_2_, ...), custom_call_target="tpu_custom_call" | custom-call | tf_op jit(solution)/shard_map/pallas_call | solution.py:166
  8.9 1.3 collective-permute-start.6
  10.2 0.7 collective-permute-start.5
  10.9 0.1 collective-permute-start.3
  11.0 0.4 collective-permute-start.4
  11.4 0.1 collective-permute-start.7
  11.5 1.3 collective-permute-done.3.refs_2_
  12.8 0.4 collective-permute-done.4.refs_7_
  13.2 0.0 collective-permute-done.5.refs_9_
  13.2 0.3 copy-done.17
  13.5 0.4 copy-done.18
  13.9 0.8 copy-done.12
  14.7 5.3 %shard_map.201 = (bf16[512,320]{1,0:T(8,128)(2,1)S(1)}, f32[320,512]{1,0:T(8,128)S(1)}, f32[320,512]{1,0:T(8,128)}, bf16[512,512]{1,0:T(8,128)(2,1)}) custom-call(bf16[320,512]{1,0:T(8,128)(2,1)} %refs_8_.2, bf16[512,256]{1,0:T(8,128)(2,1)} %refs_1_.4, bf16[512,256]{1,0:T(8,128)(2,1)} %copy-done.17, s32[3,1024]{1,0:T(4,128)} %refs_3_.5, s32[3,1024]{1,0:T(4,128)} %refs_2_.5, ...), custom_call_target="tpu_custom_call" | custom-call | tf_op jit(solution)/shard_map/pallas_call | solution.py:166
  20.0 0.0 collective-permute-done.7.refs_7_
  20.0 0.0 copy-start.14
  20.0 4.5 %collective-permute-done.6.refs_3_ = bf16[512,1024]{1,0:T(8,128)(2,1)S(1)} collective-permute-done((bf16[512,1024]{1,0:T(8,128)(2,1)S(1)}, bf16[512,1024]{1,0:T(8,128)(2,1)S(1)}, u32[]{:S(2)}, u32[]{:S(2)}) %collective-permute-start.6) | collective-permute-done | bytes 1048608 | tf_op jit(solution)/shard_map/ppermute | solution.py:372
  24.5 2.1 %shard_map.202 = (bf16[320,512]{1,0:T(8,128)(2,1)S(1)}, bf16[512,512]{1,0:T(8,128)(2,1)S(1)}, f32[320,512]{1,0:T(8,128)S(1)}, bf16[256,512]{1,0:T(8,128)(2,1)S(1...) custom-call(bf16[512,320]{1,0:T(8,128)(2,1)S(1)} %get-tuple-element.49.refs_0_, ...), custom_call_target="tpu_custom_call" | custom-call | tf_op jit(solution)/shard_map/pallas_call | solution.py:166
  26.6 0.3 collective-permute-start.8
  26.9 0.1 copy.23
  27.0 0.1 copy.24
  27.1 0.1 reshape.25.refs_8_
  27.2 1.3 collective-permute-done.8.refs_1_
  28.5 2.7 %shard_map.203 = (bf16[320,512]{1,0:T(8,128)(2,1)}, bf16[2048,256]{1,0:T(8,128)(2,1)}) custom-call(bf16[320,512]{1,0:T(8,128)(2,1)S(1)} %get-tuple-element.55.refs_0_, bf16[320,512]{1,0:T(8,128)(2,1)S(1)} %collective-permute-done.8.refs_1_, bf16[512,512]{1,0:T(8,128)(2,1)S(1)} %get-tuple-element.56.refs_2_, f32[320,512]{1,0:T(8,128)S(1)} %get-tuple-element.57.refs_3_, ...), custom_call_target="tpu_custom_call" | custom-call | tf_op jit(solution)/shard_map/pallas_call | solution.py:166
  31.2 0.0 copy-start.9
  31.2 0.0 copy-start.1
  31.2 0.0 copy-start.19
  31.2 0.0 copy-start.20
  31.2 17.7 %all-to-all-start = ((bf16[128,16,256]{2,1,0:T(8,128)(2,1)}), bf16[128,16,256]{2,1,0:T(8,128)(2,1)S(1)}, u32[]{:S(2)}, u32[]{:S(2)}) async-start(bf16[128,16,256]{2,1,0:T(8,128)(2,1)} %bitcast.10), calls=%async_computation | async-start | bytes 2097152 | tf_op jit(solution)/shard_map/all_to_all | solution.py:414
  48.9 0.5 collective-permute-start.10
  49.4 0.1 collective-permute-start.9
  49.6 0.4 collective-permute-start.12
  50.0 0.1 fusion.11
  50.1 2.4 %collective-permute-done.9.refs_8_ = bf16[2,256,512]{2,1,0:T(8,128)(2,1)S(1)} collective-permute-done((bf16[2,256,512]{2,1,0:T(8,128)(2,1)S(1)}, bf16[2,256,512]{2,1,0:T(8,128)(2,1)S(1)}, u32[]{:S(2)}, u32[]{:S(2)}) %collective-permute-start.9) | collective-permute-done | bytes 524320 | tf_op jit(solution)/shard_map/ppermute | solution.py:325
  52.5 0.0 collective-permute-done.10.refs_10_
  52.5 0.8 copy-done.10
  53.3 0.4 copy-done.8
  53.6 6.7 %shard_map.204 = (bf16[256,2560]{1,0:T(8,128)(2,1)}, f32[320,512]{1,0:T(8,128)}, bf16[512,512]{1,0:T(8,128)(2,1)}) custom-call(bf16[320,512]{1,0:T(8,128)(2,1)} %get-tuple-element.63.refs_0_.refs_6_, bf16[2,512,256]{2,1,0:T(8,128)(2,1)} %refs_1_.6, bf16[2,512,256]{2,1,0:T(8,128)(2,1)} %refs_2_.7, bf16[2,512,256]{2,1,0:T(8,128)(2,1)} %refs_3_.7, ...), custom_call_target="tpu_custom_call" | custom-call | tf_op jit(solution)/shard_map/pallas_call | solution.py:166
  60.3 0.0 copy-start
  60.4 0.0 copy-start.3
  60.4 16.6 %all-to-all-done = bf16[128,16,256]{2,1,0:T(8,128)(2,1)S(1)} async-done(((bf16[128,16,256]{2,1,0:T(8,128)(2,1)}), bf16[128,16,256]{2,1,0:T(8,128)(2,1)S(1)}, u32[]{:S(2)}, u32[]{:S(2)}) %all-to-all-start) | async-done | bytes 1048608 | tf_op jit(solution)/shard_map/all_to_all | solution.py:414
  76.9 4.6 %shard_map.205.refs_0_ = bf16[320,256]{1,0:T(8,128)(2,1)S(1)} custom-call(bf16[2048,256]{1,0:T(8,128)(2,1)S(1)} %bitcast.8, bf16[256,2560]{1,0:T(8,128)(2,1)} %get-tuple-element.66.refs_1_, s32[1,2560]{1,0:T(1,128)S(1)} %reshape.28.refs_5_.refs_2_, s32[1,2560]{1,0:T(1,128)S(1)} %reshape.29.refs_6_.refs_3_), custom_call_target="tpu_custom_call" | custom-call | tf_op jit(solution)/shard_map/pallas_call | solution.py:166
  81.6 2.2 %collective-permute-start.11 = (bf16[320,256]{1,0:T(8,128)(2,1)S(1)}, bf16[320,256]{1,0:T(8,128)(2,1)S(1)}, u32[]{:S(2)}, u32[]{:S(2)}) collective-permute-start(bf16[320,256]{1,0:T(8,128)(2,1)S(1)} %shard_map.205.refs_0_), channel_id=1, source_target_pairs={{0,1},{1,0},{2,3},{3,2},{4,5},{5,4},{6,7},{7,6},{8,9},{9,8},{10,11... | collective-permute-start | bytes 491528 | tf_op jit(solution)/shard_map/ppermute | solution.py:325
  83.8 0.0 collective-permute-done.12.refs_5_
  83.8 1.0 collective-permute-done.11.refs_1_
  84.8 2.6 %shard_map.206 = (bf16[320,512]{1,0:T(8,128)(2,1)}, bf16[2048,256]{1,0:T(8,128)(2,1)}) custom-call(bf16[320,256]{1,0:T(8,128)(2,1)S(1)} %shard_map.205.refs_0_, bf16[320,256]{1,0:T(8,128)(2,1)S(1)} %collective-permute-done.11.refs_1_, bf16[512,512]{1,0:T(8,128)(2,1)S(1)} %copy-done.7, f32[320,512]{1,0:T(8,128)S(1)} %copy-done.4, ...), custom_call_target="tpu_custom_call" | custom-call | tf_op jit(solution)/shard_map/pallas_call | solution.py:166
  87.5 8.2 %all-to-all-start.1 = ((bf16[128,16,256]{2,1,0:T(8,128)(2,1)}), bf16[128,16,256]{2,1,0:T(8,128)(2,1)S(1)}, u32[]{:S(2)}, u32[]{:S(2)}) async-start(bf16[128,16,256]{2,1,0:T(8,128)(2,1)} %bitcast.11), calls=%async_computation.1 | async-start | bytes 2097152 | tf_op jit(solution)/shard_map/all_to_all | solution.py:414
  95.7 6.7 %shard_map.207 = (bf16[256,2560]{1,0:T(8,128)(2,1)}, f32[320,512]{1,0:T(8,128)}, bf16[512,512]{1,0:T(8,128)(2,1)}) custom-call(bf16[320,512]{1,0:T(8,128)(2,1)} %get-tuple-element.71.refs_0_.refs_6_, bf16[2,512,256]{2,1,0:T(8,128)(2,1)} %refs_1_.6, bf16[2,512,256]{2,1,0:T(8,128)(2,1)} %refs_2_.7, bf16[2,512,256]{2,1,0:T(8,128)(2,1)} %refs_3_.7, ...), custom_call_target="tpu_custom_call" | custom-call | tf_op jit(solution)/shard_map/pallas_call | solution.py:166
  102.4 0.0 copy-start.2
  102.4 20.6 %all-to-all-done.1 = bf16[128,16,256]{2,1,0:T(8,128)(2,1)S(1)} async-done(((bf16[128,16,256]{2,1,0:T(8,128)(2,1)}), bf16[128,16,256]{2,1,0:T(8,128)(2,1)S(1)}, u32[]{:S(2)}, u32[]{:S(2)}) %all-to-all-start.1) | async-done | bytes 1048608 | tf_op jit(solution)/shard_map/all_to_all | solution.py:414
  123.0 4.6 %shard_map.208.refs_0_ = bf16[320,256]{1,0:T(8,128)(2,1)S(1)} custom-call(bf16[2048,256]{1,0:T(8,128)(2,1)S(1)} %bitcast.9, bf16[256,2560]{1,0:T(8,128)(2,1)} %get-tuple-element.72.refs_1_, s32[1,2560]{1,0:T(1,128)S(1)} %reshape.28.refs_5_.refs_2_, s32[1,2560]{1,0:T(1,128)S(1)} %reshape.29.refs_6_.refs_3_), custom_call_target="tpu_custom_call" | custom-call | tf_op jit(solution)/shard_map/pallas_call | solution.py:166
  127.6 2.7 %collective-permute-start.13 = (bf16[320,256]{1,0:T(8,128)(2,1)S(1)}, bf16[320,256]{1,0:T(8,128)(2,1)S(1)}, u32[]{:S(2)}, u32[]{:S(2)}) collective-permute-start(bf16[320,256]{1,0:T(8,128)(2,1)S(1)} %shard_map.208.refs_0_), channel_id=1, source_target_pairs={{0,1},{1,0},{2,3},{3,2},{4,5},{5,4},{6,7},{7,6},{8,9},{9,8},{10,11... | collective-permute-start | bytes 491528 | tf_op jit(solution)/shard_map/ppermute | solution.py:325
  130.3 1.0 collective-permute-done.13.refs_1_
  131.4 1.5 %shard_map.209 = bf16[320,512]{1,0:T(8,128)(2,1)} custom-call(bf16[320,256]{1,0:T(8,128)(2,1)S(1)} %shard_map.208.refs_0_, bf16[320,256]{1,0:T(8,128)(2,1)S(1)} %collective-permute-done.13.refs_1_, bf16[512,512]{1,0:T(8,128)(2,1)S(1)} %copy-done.6, f32[320,512]{1,0:T(8,128)S(1)} %copy-done.5, bf16[2,256,512]{2,1,0:T(8,128)(2,1)S(1)} %copy-done.1, ...), custom_call_target="tpu_custom_call" | custom-call | tf_op jit(solution)/shard_map/pallas_call | solution.py:166
  (29 shorter events, 0.1 us)
Async XLA Ops:
  0.0 5.5 %collective-permute-start.1 = (bf16[256,512]{1,0:T(8,128)(2,1)}, bf16[256,512]{1,0:T(8,128)(2,1)S(1)}, u32[]{:S(2)}, u32[]{:S(2)}) collective-permute-start(bf16[256,512]{1,0:T(8,128)(2,1)} %refs_2_.4), channel_id=1, source_target_pairs={{0,1},{1,0},{2,3},{3,2},{4,5},{5,4},{6,7},{7,6},{8,9},{9,8},{10,11... | collective-permute-start | bytes 786440 | tf_op jit(solution)/shard_map/ppermute | solution.py:325
  3.2 2.3 %collective-permute-start.2 = (bf16[512,256]{1,0:T(8,128)(2,1)}, bf16[512,256]{1,0:T(8,128)(2,1)S(1)}, u32[]{:S(2)}, u32[]{:S(2)}) collective-permute-start(bf16[512,256]{1,0:T(8,128)(2,1)} %refs_3_.4), channel_id=1, source_target_pairs={{0,1},{1,0},{2,3},{3,2},{4,5},{5,4},{6,7},{7,6},{8,9},{9,8},{10,11... | collective-permute-start | bytes 786440 | tf_op jit(solution)/shard_map/ppermute | solution.py:325
  3.2 2.3 %collective-permute-start = (bf16[474,256]{1,0:T(8,128)(2,1)}, bf16[474,256]{1,0:T(8,128)(2,1)S(1)}, u32[]{:S(2)}, u32[]{:S(2)}) collective-permute-start(bf16[474,256]{1,0:T(8,128)(2,1)} %refs_1_.3), channel_id=1, source_target_pairs={{0,1},{1,0},{2,3},{3,2},{4,5},{5,4},{6,7},{7,6},{8,9},{9,8},{10,11... | collective-permute-start | bytes 728072 | tf_op jit(solution)/shard_map/ppermute | solution.py:325
  5.6 4.7 %copy-start.11 = (bf16[1024,256]{1,0:T(8,128)(2,1)S(1)}, bf16[1024,256]{1,0:T(8,128)(2,1)}, u32[]{:S(2)}) copy-start(bf16[1024,256]{1,0:T(8,128)(2,1)} %refs_8_.1) | copy-start | bytes 1572868
  5.6 5.3 %copy-start.15 = (bf16[512,256]{1,0:T(8,128)(2,1)S(1)}, bf16[512,256]{1,0:T(8,128)(2,1)}, u32[]{:S(2)}) copy-start(bf16[512,256]{1,0:T(8,128)(2,1)} %refs_1_.4) | copy-start | bytes 786436
  5.6 5.4 %copy-start.16 = (bf16[256,512]{1,0:T(8,128)(2,1)S(1)}, bf16[256,512]{1,0:T(8,128)(2,1)}, u32[]{:S(2)}) copy-start(bf16[256,512]{1,0:T(8,128)(2,1)} %refs_6_) | copy-start | bytes 786436
  5.6 5.8 %copy-start.13 = (bf16[256,512]{1,0:T(8,128)(2,1)S(1)}, bf16[256,512]{1,0:T(8,128)(2,1)}, u32[]{:S(2)}) copy-start(bf16[256,512]{1,0:T(8,128)(2,1)} %refs_6_.1) | copy-start | bytes 786436
  8.9 15.5 %collective-permute-start.6 = (bf16[512,1024]{1,0:T(8,128)(2,1)S(1)}, bf16[512,1024]{1,0:T(8,128)(2,1)S(1)}, u32[]{:S(2)}, u32[]{:S(2)}) collective-permute-start(bf16[512,1024]{1,0:T(8,128)(2,1)S(1)} %get-tuple-element.51), channel_id=1, source_target_pairs={{0,2},{2,4},{4,6},{6,8},{8,10},{10,12},{12,14},{14,16},{16,18},{18... | collective-permute-start | bytes 3145736 | tf_op jit(solution)/shard_map/ppermute | solution.py:372
  10.2 3.0 %collective-permute-start.5 = (bf16[1024,256]{1,0:T(8,128)(2,1)S(1)}, bf16[1024,256]{1,0:T(8,128)(2,1)S(1)}, u32[]{:S(2)}, u32[]{:S(2)}) collective-permute-start(bf16[1024,256]{1,0:T(8,128)(2,1)S(1)} %copy-done.11), channel_id=1, source_target_pairs={{0,1},{1,0},{2,3},{3,2},{4,5},{5,4},{6,7},{7,6},{8,9},{9,8},{10,11... | collective-permute-start | bytes 1572872 | tf_op jit(solution)/shard_map/ppermute | solution.py:325
  10.9 1.9 %collective-permute-start.3 = (bf16[512,256]{1,0:T(8,128)(2,1)S(1)}, bf16[512,256]{1,0:T(8,128)(2,1)S(1)}, u32[]{:S(2)}, u32[]{:S(2)}) collective-permute-start(bf16[512,256]{1,0:T(8,128)(2,1)S(1)} %copy-done.15), channel_id=1, source_target_pairs={{0,1},{1,0},{2,3},{3,2},{4,5},{5,4},{6,7},{7,6},{8,9},{9,8},{10,11... | collective-permute-start | bytes 786440 | tf_op jit(solution)/shard_map/ppermute | solution.py:325
  11.0 2.2 %collective-permute-start.4 = (bf16[256,512]{1,0:T(8,128)(2,1)S(1)}, bf16[256,512]{1,0:T(8,128)(2,1)S(1)}, u32[]{:S(2)}, u32[]{:S(2)}) collective-permute-start(bf16[256,512]{1,0:T(8,128)(2,1)S(1)} %copy-done.16), channel_id=1, source_target_pairs={{0,1},{1,0},{2,3},{3,2},{4,5},{5,4},{6,7},{7,6},{8,9},{9,8},{10,11... | collective-permute-start | bytes 786440 | tf_op jit(solution)/shard_map/ppermute | solution.py:325
  11.4 8.6 %collective-permute-start.7 = (bf16[256,512]{1,0:T(8,128)(2,1)S(1)}, bf16[256,512]{1,0:T(8,128)(2,1)S(1)}, u32[]{:S(2)}, u32[]{:S(2)}) collective-permute-start(bf16[256,512]{1,0:T(8,128)(2,1)S(1)} %copy-done.13), channel_id=1, source_target_pairs={{0,1},{1,0},{2,3},{3,2},{4,5},{5,4},{6,7},{7,6},{8,9},{9,8},{10,11... | collective-permute-start | bytes 786440 | tf_op jit(solution)/shard_map/ppermute | solution.py:325
  12.8 0.7 copy-start.17
  13.2 0.7 copy-start.18
  13.9 0.8 copy-start.12
  20.0 4.5 %copy-start.14 = (bf16[256,512]{1,0:T(8,128)(2,1)}, bf16[256,512]{1,0:T(8,128)(2,1)S(1)}, u32[]{:S(2)}) copy-start(bf16[256,512]{1,0:T(8,128)(2,1)S(1)} %collective-permute-done.7.refs_7_) | copy-start | bytes 786436
  24.5 2.4 %copy-start.21 = (s32[128,16]{0,1:T(8,128)S(1)}, s32[128,16]{0,1:T(8,128)}, u32[]{:S(2)}) copy-start(s32[128,16]{0,1:T(8,128)} %param.26) | copy-start | bytes 24580
  26.6 1.9 %collective-permute-start.8 = (bf16[320,512]{1,0:T(8,128)(2,1)S(1)}, bf16[320,512]{1,0:T(8,128)(2,1)S(1)}, u32[]{:S(2)}, u32[]{:S(2)}) collective-permute-start(bf16[320,512]{1,0:T(8,128)(2,1)S(1)} %get-tuple-element.55.refs_0_), channel_id=1, source_target_pairs={{0,1},{1,0},{2,3},{3,2},{4,5},{5,4},{6,7},{7,6},{8,9},{9,8},{10,11... | collective-permute-start | bytes 983048 | tf_op jit(solution)/shard_map/ppermute | solution.py:325
  31.2 18.3 %copy-start.9 = (bf16[2,256,512]{2,1,0:T(8,128)(2,1)S(1)}, bf16[2,256,512]{2,1,0:T(8,128)(2,1)}, u32[]{:S(2)}) copy-start(bf16[2,256,512]{2,1,0:T(8,128)(2,1)} %refs_7_.5) | copy-start | bytes 1572868
  31.2 18.4 %copy-start.1 = (bf16[2,256,512]{2,1,0:T(8,128)(2,1)S(1)}, bf16[2,256,512]{2,1,0:T(8,128)(2,1)}, u32[]{:S(2)}) copy-start(bf16[2,256,512]{2,1,0:T(8,128)(2,1)} %refs_4_.7) | copy-start | bytes 1572868
  31.2 18.8 %copy-start.19 = (s32[2560]{0:T(1024)S(1)}, s32[2560]{0:T(1024)}, u32[]{:S(2)}) copy-start(s32[2560]{0:T(1024)} %param.27) | copy-start | bytes 30724
  31.2 18.8 %copy-start.20 = (s32[2560]{0:T(1024)S(1)}, s32[2560]{0:T(1024)}, u32[]{:S(2)}) copy-start(s32[2560]{0:T(1024)} %param.28) | copy-start | bytes 30724
  31.2 45.7 %all-to-all-start = ((bf16[128,16,256]{2,1,0:T(8,128)(2,1)}), bf16[128,16,256]{2,1,0:T(8,128)(2,1)S(1)}, u32[]{:S(2)}, u32[]{:S(2)}) async-start(bf16[128,16,256]{2,1,0:T(8,128)(2,1)} %bitcast.10), calls=%async_computation | async-start | bytes 2097152 | tf_op jit(solution)/shard_map/all_to_all | solution.py:414
  48.9 3.6 %collective-permute-start.10 = (bf16[2,1024,256]{2,1,0:T(8,128)(2,1)}, bf16[2,1024,256]{2,1,0:T(8,128)(2,1)S(1)}, u32[]{:S(2)}, u32[]{:S(2)}) collective-permute-start(bf16[2,1024,256]{2,1,0:T(8,128)(2,1)} %refs_9_.3), channel_id=1, source_target_pairs={{0,1},{1,0},{2,3},{3,2},{4,5},{5,4},{6,7},{7,6},{8,9},{9,8},{10,11... | collective-permute-start | bytes 3145736 | tf_op jit(solution)/shard_map/ppermute | solution.py:325
  49.4 3.0 %collective-permute-start.9 = (bf16[2,256,512]{2,1,0:T(8,128)(2,1)S(1)}, bf16[2,256,512]{2,1,0:T(8,128)(2,1)S(1)}, u32[]{:S(2)}, u32[]{:S(2)}) collective-permute-start(bf16[2,256,512]{2,1,0:T(8,128)(2,1)S(1)} %copy-done.9), channel_id=1, source_target_pairs={{0,1},{1,0},{2,3},{3,2},{4,5},{5,4},{6,7},{7,6},{8,9},{9,8},{10,11... | collective-permute-start | bytes 1572872 | tf_op jit(solution)/shard_map/ppermute | solution.py:325
  49.6 34.2 %collective-permute-start.12 = (bf16[2,256,512]{2,1,0:T(8,128)(2,1)S(1)}, bf16[2,256,512]{2,1,0:T(8,128)(2,1)S(1)}, u32[]{:S(2)}, u32[]{:S(2)}) collective-permute-start(bf16[2,256,512]{2,1,0:T(8,128)(2,1)S(1)} %copy-done.1), channel_id=1, source_target_pairs={{0,1},{1,0},{2,3},{3,2},{4,5},{5,4},{6,7},{7,6},{8,9},{9,8},{10,11... | collective-permute-start | bytes 1572872 | tf_op jit(solution)/shard_map/ppermute | solution.py:325
  52.5 0.8 copy-start.10
  52.5 1.2 copy-start.8
  60.3 24.5 %copy-start = (bf16[2,512,256]{2,1,0:T(8,128)(2,1)S(1)}, bf16[2,512,256]{2,1,0:T(8,128)(2,1)}, u32[]{:S(2)}) copy-start(bf16[2,512,256]{2,1,0:T(8,128)(2,1)} %refs_1_.6) | copy-start | bytes 1572868
  60.4 24.5 %copy-start.3 = (bf16[320,512]{1,0:T(8,128)(2,1)S(1)}, bf16[320,512]{1,0:T(8,128)(2,1)}, u32[]{:S(2)}) copy-start(bf16[320,512]{1,0:T(8,128)(2,1)} %get-tuple-element.63.refs_0_.refs_6_) | copy-start | bytes 983044
  60.4 24.4 %copy-start.7 = (bf16[512,512]{1,0:T(8,128)(2,1)S(1)}, bf16[512,512]{1,0:T(8,128)(2,1)}, u32[]{:S(2)}) copy-start(bf16[512,512]{1,0:T(8,128)(2,1)} %get-tuple-element.67.refs_2_) | copy-start | bytes 1572868
  76.9 7.9 %copy-start.4 = (f32[320,512]{1,0:T(8,128)S(1)}, f32[320,512]{1,0:T(8,128)}, u32[]{:S(2)}) copy-start(f32[320,512]{1,0:T(8,128)} %get-tuple-element.68.refs_3_) | copy-start | bytes 1966084
  81.6 3.2 %collective-permute-start.11 = (bf16[320,256]{1,0:T(8,128)(2,1)S(1)}, bf16[320,256]{1,0:T(8,128)(2,1)S(1)}, u32[]{:S(2)}, u32[]{:S(2)}) collective-permute-start(bf16[320,256]{1,0:T(8,128)(2,1)S(1)} %shard_map.205.refs_0_), channel_id=1, source_target_pairs={{0,1},{1,0},{2,3},{3,2},{4,5},{5,4},{6,7},{7,6},{8,9},{9,8},{10,11... | collective-permute-start | bytes 491528 | tf_op jit(solution)/shard_map/ppermute | solution.py:325
  87.5 35.5 %all-to-all-start.1 = ((bf16[128,16,256]{2,1,0:T(8,128)(2,1)}), bf16[128,16,256]{2,1,0:T(8,128)(2,1)S(1)}, u32[]{:S(2)}, u32[]{:S(2)}) async-start(bf16[128,16,256]{2,1,0:T(8,128)(2,1)} %bitcast.11), calls=%async_computation.1 | async-start | bytes 2097152 | tf_op jit(solution)/shard_map/all_to_all | solution.py:414
  102.4 28.9 %copy-start.2 = (bf16[320,512]{1,0:T(8,128)(2,1)S(1)}, bf16[320,512]{1,0:T(8,128)(2,1)}, u32[]{:S(2)}) copy-start(bf16[320,512]{1,0:T(8,128)(2,1)} %get-tuple-element.71.refs_0_.refs_6_) | copy-start | bytes 983044
  102.4 28.9 %copy-start.5 = (f32[320,512]{1,0:T(8,128)S(1)}, f32[320,512]{1,0:T(8,128)}, u32[]{:S(2)}) copy-start(f32[320,512]{1,0:T(8,128)} %get-tuple-element.74.refs_3_) | copy-start | bytes 1966084
  123.0 8.4 %copy-start.6 = (bf16[512,512]{1,0:T(8,128)(2,1)S(1)}, bf16[512,512]{1,0:T(8,128)(2,1)}, u32[]{:S(2)}) copy-start(bf16[512,512]{1,0:T(8,128)(2,1)} %get-tuple-element.73.refs_2_) | copy-start | bytes 1572868
  127.6 3.7 %collective-permute-start.13 = (bf16[320,256]{1,0:T(8,128)(2,1)S(1)}, bf16[320,256]{1,0:T(8,128)(2,1)S(1)}, u32[]{:S(2)}, u32[]{:S(2)}) collective-permute-start(bf16[320,256]{1,0:T(8,128)(2,1)S(1)} %shard_map.208.refs_0_), channel_id=1, source_target_pairs={{0,1},{1,0},{2,3},{3,2},{4,5},{5,4},{6,7},{7,6},{8,9},{9,8},{10,11... | collective-permute-start | bytes 491528 | tf_op jit(solution)/shard_map/ppermute | solution.py:325

commit v3 on v2

--- a/solution.py
+++ b/solution.py
@@ -225,17 +225,22 @@
 def prepare(latent, msg_own, msg_other, first_own, first_other, base_ref, fold_ref):
     width = latent.shape[1]
     firsts = (first_own, first_other)
-    base_ref.put(0, jnp.concatenate([matmul(latent, each[:width, :]) for each in firsts], axis=1))
+    base = jnp.concatenate([matmul(latent, each[:width, :]) for each in firsts], axis=1)
     fold = [
         jnp.concatenate([matmul(msg[...], each[width:, :]) for each in firsts], axis=1)
         for msg in (msg_own, msg_other)
     ]
-    fold_ref.put(0, jnp.concatenate(fold, axis=0).astype(BF16))
-
-
-def encode_mid_kernel(block, latent, receiver_own, receiver_other, grid_slots, mesh_slots, grid_proj,
-                      msg_own, msg_other, first_own, first_other, proj_ref, sum_ref, base_ref,
-                      fold_ref):
+    fold = jnp.concatenate(fold, axis=0).astype(BF16)
+    for values, ref in ((base, base_ref), (fold, fold_ref)):
+        if isinstance(ref, Outgoing):
+            ref.put(0, values)
+        else:
+            ref[...] = values
+
+
+def encode_mid_kernel(latent, receiver_own, receiver_other, grid_slots, mesh_slots, grid_proj,
+                      msg_own, msg_other, first_own, first_other, gathered_ref, pick_ref,
+                      sum_ref, base_ref, fold_ref, proj_ref):
     nodes = latent[...]
     half = receiver_own.shape[1]
     proj_ref[:half, :] = matmul(receiver_own[...], nodes, 0, 1).astype(BF16)
@@ -247,20 +252,15 @@
     ]
     incoming = matmul(grid_proj[...], pick_columns(grid_row, grid_proj.shape[1]))
     sum_ref[...] = join(incoming, mesh_row, proj_ref[...])
+    pick = pick_columns(jnp.where(low, mesh_slots[0:1, :], mesh_slots[2:3, :]), nodes.shape[0])
+    pick_ref[...] = pick
+    gathered_ref[...] = matmul(proj_ref[...], pick).astype(BF16)
     prepare(nodes, msg_own, msg_other, first_own, first_other, base_ref, fold_ref)
 
 
-def encode_far_kernel(block, mesh_proj, partial, mesh_slots, arrived, sum_ref, total_ref):
-    total_ref[...] = partial[...]
-    mesh_slots.wait()
-
-    def step(columns, index, carry):
-        low = lax.axis_index("tp") == 0
-        row = jnp.where(low, mesh_slots[0:1, columns], mesh_slots[2:3, columns])
-        total_ref[...] += join(arrived[:, columns].astype(F32), row, mesh_proj[...])
-
-    each_block(arrived.shape[1], block, step, unroll=True)
-    sum_ref[...] = total_ref[...].astype(BF16)
+def encode_far_kernel(gathered, pick, partial, arrived, sum_ref):
+    active = silu(arrived[...].astype(F32) + gathered[...].astype(F32)).astype(BF16)
+    sum_ref[...] = (partial[...] + matmul(pick[...], jnp.transpose(active))).astype(BF16)
 
 
 def node_kernel(hidden_own, hidden_other, fold, base, second_own, second_other, latent, *refs):
@@ -382,17 +382,17 @@
         return [Far(each, layer) for pair in (message, first) for each in pair]
 
     prepared = [((nodes, width), F32, 1), ((width, width), BF16, 1)]
-    mesh_proj, partial, base, fold = call(
-        functools.partial(encode_mid_kernel, block),
-        [((width, nodes), BF16, 0), ((nodes, width), F32, 0)] + prepared,
+    gathered, pick, partial, base, fold, *update, sender_w = call(
+        encode_mid_kernel,
+        [((width, slot_count), BF16, 0), ((nodes, slot_count), BF16, 0), ((nodes, width), F32, 0),
+         ((nodes, width), F32, 0), ((width, width), BF16, 0)],
         Far(mesh_latent), Far(receiver[0]), Far(receiver[1]), Far(slot_grid_row),
         Far(slot_mesh_row), grid_proj, *prepare_weights(encode_message, encode_first, None),
+        Carry(encode_second[0]), Carry(encode_second[1]), Carry(mesh_latent),
+        Carry(layer_sender, 0), extra=[pltpu.VMEM((width, nodes), BF16)],
     )
-    hidden, *update, sender_w = call(
-        functools.partial(encode_far_kernel, block), [((nodes, width), BF16, 0)], mesh_proj,
-        partial, Far(slot_mesh_row), arrived, Carry(fold), Carry(base), Carry(encode_second[0]),
-        Carry(encode_second[1]), Carry(mesh_latent), Carry(layer_sender, 0),
-        extra=[pltpu.VMEM((nodes, width), F32)],
+    (hidden,) = call(
+        encode_far_kernel, [((nodes, width), BF16, 0)], gathered, pick, partial, arrived,
     )
 
     order = (6, 5, 4, 3, 2, 1, 0)
@@ -405,6 +405,7 @@
         place += ((slot // (halo_slots << (bits - 1 - bit))) & 1) * (halo_slots << (bits - 1 - to))
     sender_row = jnp.where(slot < 0, edge_sender, place + nodes).reshape(1, -1)
     receiver_row = edge_receiver.reshape(1, -1)
+    update = [fold, base, *update]
     node_out = [((nodes, width), BF16, 1), ((bands * halo_slots, half), BF16, 4)]
 
     for layer in range(layers):

time: 133 us -> 132 us (level)
  Pallas kernels: 42 us -> 40.5 us
    pallas_call x11, Pallas kernels: 42 us -> 40.5 us  [call(): pl.pallas_call(body, out_shape=[pltpu.HBM(shape, dtype) if pieces else ja...]
  transfers between devices with their start and end apart: 16 -> 16, of which waited for: 9 -> 10; matrix products, arithmetic and copies ran while one was open for 0% -> 0% of each run, Pallas kernels for 19% -> 19%
where the time goes in v3:
time: 132 us
  waiting for transfers between devices  49.2 us (37%)
  Pallas kernels  40.5 us (31%)
  starting transfers between devices  38.4 us (29%)
  local copies, waits for them, and re-layouts  3.06 us (2%)
    pallas_call x11, Pallas kernels, call(): pl.pallas_call(body, out_shape=[pltpu.HBM(shape, dtype) if pieces else ja...  40.5 us
    all_to_all x2, waiting for transfers between devices, shards(): lax.all_to_all(outgoing.reshape(bands, halo_slots, half), 'band', split_a...  37.1 us
    all_to_all x2, starting transfers between devices, shards(): lax.all_to_all(outgoing.reshape(bands, halo_slots, half), 'band', split_a...  25.9 us
    ppermute x13, starting transfers between devices, swap(): return lax.ppermute(values, 'tp', [(0, 1), (1, 0)])  11.2 us
    ppermute x13, waiting for transfers between devices, swap(): return lax.ppermute(values, 'tp', [(0, 1), (1, 0)])  7.83 us
    ppermute x1, waiting for transfers between devices, shards(): arrived = lax.ppermute(outgoing, ('band', 'tp'), pairs)  4.28 us
    unnamed x45, local copies, waits for them, and re-layouts  2.86 us
  transfers between devices with their start and end apart: 16, of which 10 were waited for; matrix products, arithmetic and copies ran while one was open for 0% of the time, Pallas kernels for 19%

profile of v3, /device:TPU:1, one launch (start us, length us, event | category | flops | bytes accessed | tf_op | source)
XLA Modules:
  0.0 131.8 jit_solution(4618668873544672731)
XLA Ops:
  0.0 3.2 %collective-permute-start.1 = (bf16[256,512]{1,0:T(8,128)(2,1)}, bf16[256,512]{1,0:T(8,128)(2,1)S(1)}, u32[]{:S(2)}, u32[]{:S(2)}) collective-permute-start(bf16[256,512]{1,0:T(8,128)(2,1)} %refs_2_.3), channel_id=1, source_target_pairs={{0,1},{1,0},{2,3},{3,2},{4,5},{5,4},{6,7},{7,6},{8,9},{9,8},{10,11... | collective-permute-start | bytes 786440 | tf_op jit(solution)/shard_map/ppermute | solution.py:325
  3.2 0.0 collective-permute-start.2
  3.2 0.5 collective-permute-start
  3.8 1.8 %shard_map.199 = (bf16[256,1024]{1,0:T(8,128)(2,1)S(1)}, bf16[474,1024]{1,0:T(8,128)(2,1)S(1)}, bf16[256,512]{1,0:T(8,128)(2,1)S(1)}, bf16[512,256]{1,0:T(8,128)(2,1)S(1)}) custom-call(bf16[474,1024]{1,0:T(8,128)(2,1)} %bitcast.12, bf16[474,256]{1,0:T(8,128)(2,1)} %refs_1_.3, bf16[256,512]{1,0:T(8,128)(2,1)} %refs_2_.3, bf16[512,256]{1,0:T(8,128)(2,1)} %refs_3_.4), custom_call_target="tpu_custom_call" | custom-call | tf_op jit(solution)/shard_map/pallas_call | solution.py:166
  5.5 0.0 collective-permute-done.refs_2_
  5.5 0.0 collective-permute-done.1.refs_4_
  5.6 0.0 collective-permute-done.2.refs_6_
  5.6 0.0 copy-start.11
  5.6 0.0 copy-start.13
  5.6 0.0 copy-start.14
  5.6 0.0 copy-start.15
  5.6 3.3 %shard_map.200 = (bf16[512,1024]{1,0:T(8,128)(2,1)S(1)}, bf16[512,1024]{1,0:T(8,128)(2,1)S(1)}) custom-call(bf16[474,1024]{1,0:T(8,128)(2,1)S(1)} %get-tuple-element.38.refs_0_, bf16[256,1024]{1,0:T(8,128)(2,1)S(1)} %get-tuple-element.39.refs_1_, bf16[474,256]{1,0:T(8,128)(2,1)S(1)} %collective-permute-done.refs_2_, ...), custom_call_target="tpu_custom_call" | custom-call | tf_op jit(solution)/shard_map/pallas_call | solution.py:166
  8.9 1.3 collective-permute-start.7
  10.2 0.7 collective-permute-start.5
  10.9 0.1 collective-permute-start.3
  11.0 0.4 collective-permute-start.4
  11.4 0.1 collective-permute-start.6
  11.5 1.3 collective-permute-done.3.refs_2_
  12.8 0.4 collective-permute-done.4.refs_7_
  13.2 0.4 collective-permute-done.6.refs_11_
  13.6 0.0 collective-permute-done.5.refs_9_
  13.6 0.3 copy-done.17
  13.9 0.4 copy-done.18
  14.3 0.8 copy-done.12
  15.1 5.1 %shard_map.201 = (bf16[512,1024]{1,0:T(8,128)(2,1)S(1)}, bf16[320,1024]{1,0:T(8,128)(2,1)S(1)}, f32[320,512]{1,0:T(8,128)S(1)}, f32[320,512]{1,0:T(8,128)S(1)}, ...) custom-call(bf16[320,512]{1,0:T(8,128)(2,1)} %refs_12_.1, ...), custom_call_target="tpu_custom_call" | custom-call | tf_op jit(solution)/shard_map/pallas_call | solution.py:166
  20.2 4.3 %collective-permute-done.7.refs_3_ = bf16[512,1024]{1,0:T(8,128)(2,1)S(1)} collective-permute-done((bf16[512,1024]{1,0:T(8,128)(2,1)S(1)}, bf16[512,1024]{1,0:T(8,128)(2,1)S(1)}, u32[]{:S(2)}, u32[]{:S(2)}) %collective-permute-start.7) | collective-permute-done | bytes 1048608 | tf_op jit(solution)/shard_map/ppermute | solution.py:372
  24.5 0.8 shard_map.202.refs_0_
  25.3 0.3 collective-permute-start.8
  25.5 0.0 copy-done.21
  25.5 0.1 copy.23
  25.6 0.1 copy.24
  25.7 0.1 reshape.25.refs_8_
  25.8 1.3 collective-permute-done.8.refs_1_
  27.2 2.7 %shard_map.203 = (bf16[320,512]{1,0:T(8,128)(2,1)}, bf16[2048,256]{1,0:T(8,128)(2,1)}) custom-call(bf16[320,512]{1,0:T(8,128)(2,1)S(1)} %shard_map.202.refs_0_, bf16[320,512]{1,0:T(8,128)(2,1)S(1)} %collective-permute-done.8.refs_1_, bf16[512,512]{1,0:T(8,128)(2,1)S(1)} %get-tuple-element.52.refs_2_, f32[320,512]{1,0:T(8,128)S(1)} %get-tuple-element.53.refs_3_, ...), custom_call_target="tpu_custom_call" | custom-call | tf_op jit(solution)/shard_map/pallas_call | solution.py:166
  29.8 0.0 copy-start.9
  29.9 0.0 copy-start.1
  29.9 0.0 copy-start.19
  29.9 0.0 copy-start.20
  29.9 17.7 %all-to-all-start = ((bf16[128,16,256]{2,1,0:T(8,128)(2,1)}), bf16[128,16,256]{2,1,0:T(8,128)(2,1)S(1)}, u32[]{:S(2)}, u32[]{:S(2)}) async-start(bf16[128,16,256]{2,1,0:T(8,128)(2,1)} %bitcast.10), calls=%async_computation | async-start | bytes 2097152 | tf_op jit(solution)/shard_map/all_to_all | solution.py:415
  47.6 0.5 collective-permute-start.10
  48.1 0.1 collective-permute-start.9
  48.2 0.4 collective-permute-start.12
  48.6 0.1 fusion.11
  48.7 2.4 %collective-permute-done.9.refs_8_ = bf16[2,256,512]{2,1,0:T(8,128)(2,1)S(1)} collective-permute-done((bf16[2,256,512]{2,1,0:T(8,128)(2,1)S(1)}, bf16[2,256,512]{2,1,0:T(8,128)(2,1)S(1)}, u32[]{:S(2)}, u32[]{:S(2)}) %collective-permute-start.9) | collective-permute-done | bytes 524320 | tf_op jit(solution)/shard_map/ppermute | solution.py:325
  51.1 0.0 collective-permute-done.10.refs_10_
  51.1 0.8 copy-done.10
  51.9 0.4 copy-done.8
  52.3 6.7 %shard_map.204 = (bf16[256,2560]{1,0:T(8,128)(2,1)}, f32[320,512]{1,0:T(8,128)}, bf16[512,512]{1,0:T(8,128)(2,1)}) custom-call(bf16[320,512]{1,0:T(8,128)(2,1)} %get-tuple-element.59.refs_0_.refs_6_, bf16[2,512,256]{2,1,0:T(8,128)(2,1)} %refs_1_.6, bf16[2,512,256]{2,1,0:T(8,128)(2,1)} %refs_2_.5, bf16[2,512,256]{2,1,0:T(8,128)(2,1)} %refs_3_.7, ...), custom_call_target="tpu_custom_call" | custom-call | tf_op jit(solution)/shard_map/pallas_call | solution.py:166
  59.0 0.0 copy-start
  59.0 0.0 copy-start.3
  59.1 16.6 %all-to-all-done = bf16[128,16,256]{2,1,0:T(8,128)(2,1)S(1)} async-done(((bf16[128,16,256]{2,1,0:T(8,128)(2,1)}), bf16[128,16,256]{2,1,0:T(8,128)(2,1)S(1)}, u32[]{:S(2)}, u32[]{:S(2)}) %all-to-all-start) | async-done | bytes 1048608 | tf_op jit(solution)/shard_map/all_to_all | solution.py:415
  75.6 4.6 %shard_map.205.refs_0_ = bf16[320,256]{1,0:T(8,128)(2,1)S(1)} custom-call(bf16[2048,256]{1,0:T(8,128)(2,1)S(1)} %bitcast.8, bf16[256,2560]{1,0:T(8,128)(2,1)} %get-tuple-element.62.refs_1_, s32[1,2560]{1,0:T(1,128)S(1)} %reshape.28.refs_5_.refs_2_, s32[1,2560]{1,0:T(1,128)S(1)} %reshape.29.refs_6_.refs_3_), custom_call_target="tpu_custom_call" | custom-call | tf_op jit(solution)/shard_map/pallas_call | solution.py:166
  80.3 2.2 %collective-permute-start.11 = (bf16[320,256]{1,0:T(8,128)(2,1)S(1)}, bf16[320,256]{1,0:T(8,128)(2,1)S(1)}, u32[]{:S(2)}, u32[]{:S(2)}) collective-permute-start(bf16[320,256]{1,0:T(8,128)(2,1)S(1)} %shard_map.205.refs_0_), channel_id=1, source_target_pairs={{0,1},{1,0},{2,3},{3,2},{4,5},{5,4},{6,7},{7,6},{8,9},{9,8},{10,11... | collective-permute-start | bytes 491528 | tf_op jit(solution)/shard_map/ppermute | solution.py:325
  82.4 0.0 collective-permute-done.12.refs_5_
  82.4 1.0 collective-permute-done.11.refs_1_
  83.5 2.7 %shard_map.206 = (bf16[320,512]{1,0:T(8,128)(2,1)}, bf16[2048,256]{1,0:T(8,128)(2,1)}) custom-call(bf16[320,256]{1,0:T(8,128)(2,1)S(1)} %shard_map.205.refs_0_, bf16[320,256]{1,0:T(8,128)(2,1)S(1)} %collective-permute-done.11.refs_1_, bf16[512,512]{1,0:T(8,128)(2,1)S(1)} %copy-done.7, f32[320,512]{1,0:T(8,128)S(1)} %copy-done.4, ...), custom_call_target="tpu_custom_call" | custom-call | tf_op jit(solution)/shard_map/pallas_call | solution.py:166
  86.2 8.2 %all-to-all-start.1 = ((bf16[128,16,256]{2,1,0:T(8,128)(2,1)}), bf16[128,16,256]{2,1,0:T(8,128)(2,1)S(1)}, u32[]{:S(2)}, u32[]{:S(2)}) async-start(bf16[128,16,256]{2,1,0:T(8,128)(2,1)} %bitcast.11), calls=%async_computation.1 | async-start | bytes 2097152 | tf_op jit(solution)/shard_map/all_to_all | solution.py:415
  94.4 6.7 %shard_map.207 = (bf16[256,2560]{1,0:T(8,128)(2,1)}, f32[320,512]{1,0:T(8,128)}, bf16[512,512]{1,0:T(8,128)(2,1)}) custom-call(bf16[320,512]{1,0:T(8,128)(2,1)} %get-tuple-element.67.refs_0_.refs_6_, bf16[2,512,256]{2,1,0:T(8,128)(2,1)} %refs_1_.6, bf16[2,512,256]{2,1,0:T(8,128)(2,1)} %refs_2_.5, bf16[2,512,256]{2,1,0:T(8,128)(2,1)} %refs_3_.7, ...), custom_call_target="tpu_custom_call" | custom-call | tf_op jit(solution)/shard_map/pallas_call | solution.py:166
  101.1 0.0 copy-start.2
  101.1 20.6 %all-to-all-done.1 = bf16[128,16,256]{2,1,0:T(8,128)(2,1)S(1)} async-done(((bf16[128,16,256]{2,1,0:T(8,128)(2,1)}), bf16[128,16,256]{2,1,0:T(8,128)(2,1)S(1)}, u32[]{:S(2)}, u32[]{:S(2)}) %all-to-all-start.1) | async-done | bytes 1048608 | tf_op jit(solution)/shard_map/all_to_all | solution.py:415
  121.7 4.6 %shard_map.208.refs_0_ = bf16[320,256]{1,0:T(8,128)(2,1)S(1)} custom-call(bf16[2048,256]{1,0:T(8,128)(2,1)S(1)} %bitcast.9, bf16[256,2560]{1,0:T(8,128)(2,1)} %get-tuple-element.68.refs_1_, s32[1,2560]{1,0:T(1,128)S(1)} %reshape.28.refs_5_.refs_2_, s32[1,2560]{1,0:T(1,128)S(1)} %reshape.29.refs_6_.refs_3_), custom_call_target="tpu_custom_call" | custom-call | tf_op jit(solution)/shard_map/pallas_call | solution.py:166
  126.3 2.7 %collective-permute-start.13 = (bf16[320,256]{1,0:T(8,128)(2,1)S(1)}, bf16[320,256]{1,0:T(8,128)(2,1)S(1)}, u32[]{:S(2)}, u32[]{:S(2)}) collective-permute-start(bf16[320,256]{1,0:T(8,128)(2,1)S(1)} %shard_map.208.refs_0_), channel_id=1, source_target_pairs={{0,1},{1,0},{2,3},{3,2},{4,5},{5,4},{6,7},{7,6},{8,9},{9,8},{10,11... | collective-permute-start | bytes 491528 | tf_op jit(solution)/shard_map/ppermute | solution.py:325
  129.0 1.0 collective-permute-done.13.refs_1_
  130.1 1.5 %shard_map.209 = bf16[320,512]{1,0:T(8,128)(2,1)} custom-call(bf16[320,256]{1,0:T(8,128)(2,1)S(1)} %shard_map.208.refs_0_, bf16[320,256]{1,0:T(8,128)(2,1)S(1)} %collective-permute-done.13.refs_1_, bf16[512,512]{1,0:T(8,128)(2,1)S(1)} %copy-done.6, f32[320,512]{1,0:T(8,128)S(1)} %copy-done.5, bf16[2,256,512]{2,1,0:T(8,128)(2,1)S(1)} %copy-done.1, ...), custom_call_target="tpu_custom_call" | custom-call | tf_op jit(solution)/shard_map/pallas_call | solution.py:166
  (29 shorter events, 0.1 us)
Async XLA Ops:
  0.0 5.5 %collective-permute-start.1 = (bf16[256,512]{1,0:T(8,128)(2,1)}, bf16[256,512]{1,0:T(8,128)(2,1)S(1)}, u32[]{:S(2)}, u32[]{:S(2)}) collective-permute-start(bf16[256,512]{1,0:T(8,128)(2,1)} %refs_2_.3), channel_id=1, source_target_pairs={{0,1},{1,0},{2,3},{3,2},{4,5},{5,4},{6,7},{7,6},{8,9},{9,8},{10,11... | collective-permute-start | bytes 786440 | tf_op jit(solution)/shard_map/ppermute | solution.py:325
  3.2 2.3 %collective-permute-start.2 = (bf16[512,256]{1,0:T(8,128)(2,1)}, bf16[512,256]{1,0:T(8,128)(2,1)S(1)}, u32[]{:S(2)}, u32[]{:S(2)}) collective-permute-start(bf16[512,256]{1,0:T(8,128)(2,1)} %refs_3_.4), channel_id=1, source_target_pairs={{0,1},{1,0},{2,3},{3,2},{4,5},{5,4},{6,7},{7,6},{8,9},{9,8},{10,11... | collective-permute-start | bytes 786440 | tf_op jit(solution)/shard_map/ppermute | solution.py:325
  3.2 2.3 %collective-permute-start = (bf16[474,256]{1,0:T(8,128)(2,1)}, bf16[474,256]{1,0:T(8,128)(2,1)S(1)}, u32[]{:S(2)}, u32[]{:S(2)}) collective-permute-start(bf16[474,256]{1,0:T(8,128)(2,1)} %refs_1_.3), channel_id=1, source_target_pairs={{0,1},{1,0},{2,3},{3,2},{4,5},{5,4},{6,7},{7,6},{8,9},{9,8},{10,11... | collective-permute-start | bytes 728072 | tf_op jit(solution)/shard_map/ppermute | solution.py:325
  5.6 4.7 %copy-start.11 = (bf16[1024,256]{1,0:T(8,128)(2,1)S(1)}, bf16[1024,256]{1,0:T(8,128)(2,1)}, u32[]{:S(2)}) copy-start(bf16[1024,256]{1,0:T(8,128)(2,1)} %refs_8_) | copy-start | bytes 1572868
  5.6 5.3 %copy-start.13 = (bf16[512,256]{1,0:T(8,128)(2,1)S(1)}, bf16[512,256]{1,0:T(8,128)(2,1)}, u32[]{:S(2)}) copy-start(bf16[512,256]{1,0:T(8,128)(2,1)} %refs_1_.4) | copy-start | bytes 786436
  5.6 5.4 %copy-start.14 = (bf16[256,512]{1,0:T(8,128)(2,1)S(1)}, bf16[256,512]{1,0:T(8,128)(2,1)}, u32[]{:S(2)}) copy-start(bf16[256,512]{1,0:T(8,128)(2,1)} %refs_6_) | copy-start | bytes 786436
  5.6 5.8 %copy-start.15 = (bf16[256,512]{1,0:T(8,128)(2,1)S(1)}, bf16[256,512]{1,0:T(8,128)(2,1)}, u32[]{:S(2)}) copy-start(bf16[256,512]{1,0:T(8,128)(2,1)} %refs_10_) | copy-start | bytes 786436
  8.9 15.5 %collective-permute-start.7 = (bf16[512,1024]{1,0:T(8,128)(2,1)S(1)}, bf16[512,1024]{1,0:T(8,128)(2,1)S(1)}, u32[]{:S(2)}, u32[]{:S(2)}) collective-permute-start(bf16[512,1024]{1,0:T(8,128)(2,1)S(1)} %get-tuple-element.51), channel_id=1, source_target_pairs={{0,2},{2,4},{4,6},{6,8},{8,10},{10,12},{12,14},{14,16},{16,18},{18... | collective-permute-start | bytes 3145736 | tf_op jit(solution)/shard_map/ppermute | solution.py:372
  10.2 3.3 %collective-permute-start.5 = (bf16[1024,256]{1,0:T(8,128)(2,1)S(1)}, bf16[1024,256]{1,0:T(8,128)(2,1)S(1)}, u32[]{:S(2)}, u32[]{:S(2)}) collective-permute-start(bf16[1024,256]{1,0:T(8,128)(2,1)S(1)} %copy-done.11), channel_id=1, source_target_pairs={{0,1},{1,0},{2,3},{3,2},{4,5},{5,4},{6,7},{7,6},{8,9},{9,8},{10,11... | collective-permute-start | bytes 1572872 | tf_op jit(solution)/shard_map/ppermute | solution.py:325
  10.9 1.9 %collective-permute-start.3 = (bf16[512,256]{1,0:T(8,128)(2,1)S(1)}, bf16[512,256]{1,0:T(8,128)(2,1)S(1)}, u32[]{:S(2)}, u32[]{:S(2)}) collective-permute-start(bf16[512,256]{1,0:T(8,128)(2,1)S(1)} %copy-done.13), channel_id=1, source_target_pairs={{0,1},{1,0},{2,3},{3,2},{4,5},{5,4},{6,7},{7,6},{8,9},{9,8},{10,11... | collective-permute-start | bytes 786440 | tf_op jit(solution)/shard_map/ppermute | solution.py:325
  11.0 2.2 %collective-permute-start.4 = (bf16[256,512]{1,0:T(8,128)(2,1)S(1)}, bf16[256,512]{1,0:T(8,128)(2,1)S(1)}, u32[]{:S(2)}, u32[]{:S(2)}) collective-permute-start(bf16[256,512]{1,0:T(8,128)(2,1)S(1)} %copy-done.14), channel_id=1, source_target_pairs={{0,1},{1,0},{2,3},{3,2},{4,5},{5,4},{6,7},{7,6},{8,9},{9,8},{10,11... | collective-permute-start | bytes 786440 | tf_op jit(solution)/shard_map/ppermute | solution.py:325
  11.4 2.1 %collective-permute-start.6 = (bf16[256,512]{1,0:T(8,128)(2,1)S(1)}, bf16[256,512]{1,0:T(8,128)(2,1)S(1)}, u32[]{:S(2)}, u32[]{:S(2)}) collective-permute-start(bf16[256,512]{1,0:T(8,128)(2,1)S(1)} %copy-done.15), channel_id=1, source_target_pairs={{0,1},{1,0},{2,3},{3,2},{4,5},{5,4},{6,7},{7,6},{8,9},{9,8},{10,11... | collective-permute-start | bytes 786440 | tf_op jit(solution)/shard_map/ppermute | solution.py:325
  12.8 0.8 copy-start.16
  13.2 0.7 copy-start.17
  13.6 0.7 copy-start.18
  14.3 0.8 copy-start.12
  24.5 1.1 copy-start.21
  25.3 1.9 %collective-permute-start.8 = (bf16[320,512]{1,0:T(8,128)(2,1)S(1)}, bf16[320,512]{1,0:T(8,128)(2,1)S(1)}, u32[]{:S(2)}, u32[]{:S(2)}) collective-permute-start(bf16[320,512]{1,0:T(8,128)(2,1)S(1)} %shard_map.202.refs_0_), channel_id=1, source_target_pairs={{0,1},{1,0},{2,3},{3,2},{4,5},{5,4},{6,7},{7,6},{8,9},{9,8},{10,11... | collective-permute-start | bytes 983048 | tf_op jit(solution)/shard_map/ppermute | solution.py:325
  29.8 18.3 %copy-start.9 = (bf16[2,256,512]{2,1,0:T(8,128)(2,1)S(1)}, bf16[2,256,512]{2,1,0:T(8,128)(2,1)}, u32[]{:S(2)}) copy-start(bf16[2,256,512]{2,1,0:T(8,128)(2,1)} %refs_7_.5) | copy-start | bytes 1572868
  29.9 18.4 %copy-start.1 = (bf16[2,256,512]{2,1,0:T(8,128)(2,1)S(1)}, bf16[2,256,512]{2,1,0:T(8,128)(2,1)}, u32[]{:S(2)}) copy-start(bf16[2,256,512]{2,1,0:T(8,128)(2,1)} %refs_4_.7) | copy-start | bytes 1572868
  29.9 18.8 %copy-start.19 = (s32[2560]{0:T(1024)S(1)}, s32[2560]{0:T(1024)}, u32[]{:S(2)}) copy-start(s32[2560]{0:T(1024)} %param.27) | copy-start | bytes 30724
  29.9 18.8 %copy-start.20 = (s32[2560]{0:T(1024)S(1)}, s32[2560]{0:T(1024)}, u32[]{:S(2)}) copy-start(s32[2560]{0:T(1024)} %param.28) | copy-start | bytes 30724
  29.9 45.7 %all-to-all-start = ((bf16[128,16,256]{2,1,0:T(8,128)(2,1)}), bf16[128,16,256]{2,1,0:T(8,128)(2,1)S(1)}, u32[]{:S(2)}, u32[]{:S(2)}) async-start(bf16[128,16,256]{2,1,0:T(8,128)(2,1)} %bitcast.10), calls=%async_computation | async-start | bytes 2097152 | tf_op jit(solution)/shard_map/all_to_all | solution.py:415
  47.6 3.6 %collective-permute-start.10 = (bf16[2,1024,256]{2,1,0:T(8,128)(2,1)}, bf16[2,1024,256]{2,1,0:T(8,128)(2,1)S(1)}, u32[]{:S(2)}, u32[]{:S(2)}) collective-permute-start(bf16[2,1024,256]{2,1,0:T(8,128)(2,1)} %refs_9_.1), channel_id=1, source_target_pairs={{0,1},{1,0},{2,3},{3,2},{4,5},{5,4},{6,7},{7,6},{8,9},{9,8},{10,11... | collective-permute-start | bytes 3145736 | tf_op jit(solution)/shard_map/ppermute | solution.py:325
  48.1 3.0 %collective-permute-start.9 = (bf16[2,256,512]{2,1,0:T(8,128)(2,1)S(1)}, bf16[2,256,512]{2,1,0:T(8,128)(2,1)S(1)}, u32[]{:S(2)}, u32[]{:S(2)}) collective-permute-start(bf16[2,256,512]{2,1,0:T(8,128)(2,1)S(1)} %copy-done.9), channel_id=1, source_target_pairs={{0,1},{1,0},{2,3},{3,2},{4,5},{5,4},{6,7},{7,6},{8,9},{9,8},{10,11... | collective-permute-start | bytes 1572872 | tf_op jit(solution)/shard_map/ppermute | solution.py:325
  48.2 34.2 %collective-permute-start.12 = (bf16[2,256,512]{2,1,0:T(8,128)(2,1)S(1)}, bf16[2,256,512]{2,1,0:T(8,128)(2,1)S(1)}, u32[]{:S(2)}, u32[]{:S(2)}) collective-permute-start(bf16[2,256,512]{2,1,0:T(8,128)(2,1)S(1)} %copy-done.1), channel_id=1, source_target_pairs={{0,1},{1,0},{2,3},{3,2},{4,5},{5,4},{6,7},{7,6},{8,9},{9,8},{10,11... | collective-permute-start | bytes 1572872 | tf_op jit(solution)/shard_map/ppermute | solution.py:325
  51.1 0.8 copy-start.10
  51.1 1.2 copy-start.8
  59.0 24.5 %copy-start = (bf16[2,512,256]{2,1,0:T(8,128)(2,1)S(1)}, bf16[2,512,256]{2,1,0:T(8,128)(2,1)}, u32[]{:S(2)}) copy-start(bf16[2,512,256]{2,1,0:T(8,128)(2,1)} %refs_1_.6) | copy-start | bytes 1572868
  59.0 24.4 %copy-start.3 = (bf16[320,512]{1,0:T(8,128)(2,1)S(1)}, bf16[320,512]{1,0:T(8,128)(2,1)}, u32[]{:S(2)}) copy-start(bf16[320,512]{1,0:T(8,128)(2,1)} %get-tuple-element.59.refs_0_.refs_6_) | copy-start | bytes 983044
  59.0 24.4 %copy-start.7 = (bf16[512,512]{1,0:T(8,128)(2,1)S(1)}, bf16[512,512]{1,0:T(8,128)(2,1)}, u32[]{:S(2)}) copy-start(bf16[512,512]{1,0:T(8,128)(2,1)} %get-tuple-element.63.refs_2_) | copy-start | bytes 1572868
  75.6 7.9 %copy-start.4 = (f32[320,512]{1,0:T(8,128)S(1)}, f32[320,512]{1,0:T(8,128)}, u32[]{:S(2)}) copy-start(f32[320,512]{1,0:T(8,128)} %get-tuple-element.64.refs_3_) | copy-start | bytes 1966084
  80.3 3.2 %collective-permute-start.11 = (bf16[320,256]{1,0:T(8,128)(2,1)S(1)}, bf16[320,256]{1,0:T(8,128)(2,1)S(1)}, u32[]{:S(2)}, u32[]{:S(2)}) collective-permute-start(bf16[320,256]{1,0:T(8,128)(2,1)S(1)} %shard_map.205.refs_0_), channel_id=1, source_target_pairs={{0,1},{1,0},{2,3},{3,2},{4,5},{5,4},{6,7},{7,6},{8,9},{9,8},{10,11... | collective-permute-start | bytes 491528 | tf_op jit(solution)/shard_map/ppermute | solution.py:325
  86.2 35.5 %all-to-all-start.1 = ((bf16[128,16,256]{2,1,0:T(8,128)(2,1)}), bf16[128,16,256]{2,1,0:T(8,128)(2,1)S(1)}, u32[]{:S(2)}, u32[]{:S(2)}) async-start(bf16[128,16,256]{2,1,0:T(8,128)(2,1)} %bitcast.11), calls=%async_computation.1 | async-start | bytes 2097152 | tf_op jit(solution)/shard_map/all_to_all | solution.py:415
  101.1 29.0 %copy-start.2 = (bf16[320,512]{1,0:T(8,128)(2,1)S(1)}, bf16[320,512]{1,0:T(8,128)(2,1)}, u32[]{:S(2)}) copy-start(bf16[320,512]{1,0:T(8,128)(2,1)} %get-tuple-element.67.refs_0_.refs_6_) | copy-start | bytes 983044
  101.1 28.9 %copy-start.5 = (f32[320,512]{1,0:T(8,128)S(1)}, f32[320,512]{1,0:T(8,128)}, u32[]{:S(2)}) copy-start(f32[320,512]{1,0:T(8,128)} %get-tuple-element.70.refs_3_) | copy-start | bytes 1966084
  121.7 8.4 %copy-start.6 = (bf16[512,512]{1,0:T(8,128)(2,1)S(1)}, bf16[512,512]{1,0:T(8,128)(2,1)}, u32[]{:S(2)}) copy-start(bf16[512,512]{1,0:T(8,128)(2,1)} %get-tuple-element.69.refs_2_) | copy-start | bytes 1572868
  126.3 3.7 %collective-permute-start.13 = (bf16[320,256]{1,0:T(8,128)(2,1)S(1)}, bf16[320,256]{1,0:T(8,128)(2,1)S(1)}, u32[]{:S(2)}, u32[]{:S(2)}) collective-permute-start(bf16[320,256]{1,0:T(8,128)(2,1)S(1)} %shard_map.208.refs_0_), channel_id=1, source_target_pairs={{0,1},{1,0},{2,3},{3,2},{4,5},{5,4},{6,7},{7,6},{8,9},{9,8},{10,11... | collective-permute-start | bytes 491528 | tf_op jit(solution)/shard_map/ppermute | solution.py:325
